TPU v7x, 32 devices: a whole 2x2x4 slice. The times are simulated.
32 devices in a mesh: dp: 8 (over z, x), mp: 4 (over y, core).
Axes of the slice: x: 2, y: 2, z: 4, core: 2. Of those that a mesh axis runs over, the one named last changes fastest.
Arguments:
- queries: bfloat16 [8, 512, 2048], P('dp', 'mp'), may hold values from -6 to 6
- keys: bfloat16 [8, 512, 1024], P('dp'), may hold values from -6 to 6
- values: bfloat16 [8, 512, 1024], P('dp'), may hold values from -6 to 6
- stream: bfloat16 [8, 512, 3584], P('dp', None, 'mp'), may hold values from -6 to 6
- out_proj: bfloat16 [2048, 3584], P(None, 'mp'), may hold values from -0.125 to 0.125
- norm_gain: float32 [3584], P('mp'), may hold values from 0.1 to 1.9
- tag_proj: bfloat16 [3584, 128], P('mp'), may hold values from -0.03125 to 0.03125
- direction: float32 [2048, 3584], P('dp', 'mp'), may hold values from -120 to 120
- starts: int32 [8, 4], P('dp'), may hold values from 0 to 511, as said below
- tags: int32 [8, 512], P('dp'), may hold values from 0 to 127
Outputs:
- iterate: float32 [2048, 3584], P('dp', 'mp')
Inputs may be any that keep to these rules, and one draw needn't show every extreme that they name: `starts`: each sequence's first entry is 0 and the entries rise strictly, so every file holds one token or more.
All inputs are finite; a program needn't handle non-finite values.
Results may differ from a plain program's by a relative error of at most 0.0032.
Values may be sent and summed in bfloat16 or wider, within the bound.
A program may use at most 64 MiB of HBM per device.

v0:
```python
import jax
import jax.numpy as jnp
from jax import lax
from jax.sharding import PartitionSpec as P

D = 3584
HD = 256
HQ = 8
HK = 4
TAGS = 128
WINDOW = 256
ITERS = 2


DAMP = 0.01
NORM_EPS = 1e-06
MEAN_EPS = 1e-06


def attend(query, key, value, start, offset):
    num_q = query.shape[0]
    num_k = key.shape[0]
    group = HQ // HK
    q_heads = query.reshape(num_q, HK, group, HD)
    k_heads = key.reshape(num_k, HK, HD)
    v_heads = value.reshape(num_k, HK, HD)
    scores = jnp.einsum(
        "qgrd,kgd->grqk", q_heads, k_heads, preferred_element_type=jnp.float32
    ) / jnp.sqrt(jnp.float32(HD))
    scores = 50.0 * jnp.tanh(scores / 50.0)
    q_pos = offset + jnp.arange(num_q, dtype=jnp.int32)
    k_pos = jnp.arange(num_k, dtype=jnp.int32)
    q_file = jnp.sum((start[None, :] <= q_pos[:, None]).astype(jnp.int32), 1) - 1
    k_file = jnp.sum((start[None, :] <= k_pos[:, None]).astype(jnp.int32), 1) - 1
    allowed = (
        (q_file[:, None] == k_file[None, :])
        & (k_pos[None, :] <= q_pos[:, None])
        & (q_pos[:, None] - k_pos[None, :] < WINDOW)
    )
    expo = jnp.where(allowed[None, None], jnp.exp(scores), 0.0)
    weights = (expo / jnp.sum(expo, -1, keepdims=True)).astype(jnp.bfloat16)
    out = jnp.einsum("grqk,kgd->qgrd", weights, v_heads, preferred_element_type=jnp.float32)
    return out.reshape(num_q, HQ * HD).astype(jnp.bfloat16)


def local(queries, keys, values, stream, out_proj, norm_gain, tag_proj, direction, starts, tags):
    q_rows = queries.shape[1]
    offset = lax.axis_index("mp") * q_rows
    local_out = attend(queries[0], keys[0], values[0], starts[0], offset)
    attn = lax.all_gather(local_out[None], "mp", axis=1, tiled=True)[0]
    count = HQ * HD * D
    early_norm = lax.psum(jnp.sum(direction * direction), ("dp", "mp"))
    h_loc = stream[0].astype(jnp.float32) + jnp.dot(
        attn, out_proj, preferred_element_type=jnp.float32
    )
    wide = tag_proj.astype(jnp.float32)
    sumsq, zval = lax.psum(
        (
            jnp.sum(h_loc * h_loc, -1),
            jnp.dot(h_loc * norm_gain, wide, precision=lax.Precision.HIGHEST),
        ),
        "mp",
    )
    rscale = (sumsq / D + NORM_EPS) ** (-0.5)
    tanh_val = jnp.tanh(rscale[:, None] * zval / 30.0)
    slope = 1.0 - tanh_val * tanh_val
    expo = jnp.exp(30.0 * tanh_val)
    probs = expo / jnp.sum(expo, -1, keepdims=True)
    onehot = (tags[0][:, None] == jnp.arange(TAGS, dtype=jnp.int32)[None, :]).astype(jnp.float32)
    dlogit = probs - onehot
    wgrad = dlogit * slope
    rho = jnp.sum(wgrad * zval, -1)
    cube = rscale**3 / D
    sigma = jnp.float32(1.0)
    current = direction
    for step in range(ITERS):
        hdot = jnp.dot(
            attn,
            lax.all_gather(current.astype(jnp.bfloat16), "dp", axis=0, tiled=True),
            preferred_element_type=jnp.float32,
        )
        along, zdot = lax.psum(
            (
                jnp.sum(h_loc * hdot, -1),
                jnp.dot(hdot * norm_gain, wide, precision=lax.Precision.HIGHEST),
            ),
            "mp",
        )
        rdot = -cube * along
        mdot = rdot[:, None] * zval + rscale[:, None] * zdot
        ldot = slope * mdot
        pdot = probs * (ldot - jnp.sum(probs * ldot, -1, keepdims=True))
        wdot = pdot * slope - dlogit * 2.0 * tanh_val * slope * mdot / 30.0
        rhodot = jnp.sum(wdot * zval + wgrad * zdot, -1)
        mixed = rdot[:, None] * wgrad + rscale[:, None] * wdot
        back = jnp.dot(mixed, wide.T, precision=lax.Precision.HIGHEST) * norm_gain
        coeff = rhodot * cube + 3.0 * rho * rscale * rscale * rdot / D
        curvature_gdot = back - coeff[:, None] * h_loc - (rho * cube)[:, None] * hdot
        gdot = curvature_gdot.astype(jnp.bfloat16)
        hvp_rows = lax.psum_scatter(
            lax.dot_general(
                attn, gdot, (((0,), (0,)), ((), ())), preferred_element_type=jnp.float32
            ),
            "dp",
            scatter_dimension=0,
            tiled=True,
        )
        if step == 0:
            product_sq = lax.psum(jnp.sum(hvp_rows * hvp_rows), ("dp", "mp"))
            sigma = 2.0 * jnp.sqrt(
                (product_sq / count + MEAN_EPS) / (early_norm / count + MEAN_EPS)
            )
        current = direction + (1.0 - DAMP) * current - hvp_rows / sigma
    return current


def solution(mesh):
    return jax.shard_map(
        local,
        mesh=mesh,
        in_specs=(
            P("dp", "mp", None),
            P("dp", None, None),
            P("dp", None, None),
            P("dp", None, "mp"),
            P(None, "mp"),
            P("mp"),
            P("mp", None),
            P("dp", "mp"),
            P("dp", None),
            P("dp", None),
        ),
        out_specs=P("dp", "mp"),
        check_vma=False,
    )
```

profile of v0, /device:TPU:0, one launch (start us, length us, event | category | flops | bytes accessed | tf_op | source)
XLA Modules:
  0.0 616.1 jit_solution(10954339456274760450)
XLA Ops:
  9.6 2.7 reshape_squeeze.9
  13.2 3.4 bitcast_select_fusion
  16.5 2.9 fusion.18
  22.4 23.8 %all-gather.4.cloned.1.call-done = bf16[1,512,2048]{1,2,0:T(8,128)(2,1)} async-done(((bf16[1,128,2048]{1,2,0:T(8,128)(2,1)}), bf16[1,512,2048]{1,2,0:T(8,128)(2,1)}) %all-gather.4.cloned.1.call-update) | async-done | bytes 2097168 | tf_op jit(solution)/shard_map/all_gather | solution.py:50
  46.2 69.0 %all-gather.6.cloned.1.call-done = bf16[2048,896]{1,0:T(8,128)(2,1)} async-done(((bf16[256,896]{1,0:T(8,128)(2,1)}), bf16[2048,896]{1,0:T(8,128)(2,1)}) %all-gather.6.cloned.1.call-update) | async-done | bytes 3670032 | tf_op jit(solution)/shard_map/all_gather | solution.py:79
  115.2 5.2 fusion.6
  122.8 2.6 multiply_reduce_fusion.1
  127.2 5.8 all-reduce.1
  133.0 25.9 %all-reduce.8.cloned.1.call-done = (f32[512,128]{1,0:T(8,128)}, f32[512,128]{1,0:T(8,128)}) async-done(((f32[512,128]{1,0:T(8,128)}, f32[512,128]{1,0:T(8,128)}), (f32[512,128]{1,0:T(8,128)}, f32[512,128]{1,0:T(8,128)})) %all-reduce.8.cloned.1.call-update) | async-done | bytes 524304 | tf_op jit(solution)/shard_map/psum | solution.py:82
  163.1 3.2 subtract_convert_fusion.1
  166.4 5.3 fusion.4
  171.7 132.8 %reduce-scatter.3.cloned.1.call-done = f32[256,896]{1,0:T(8,128)} async-done(((f32[2048,896]{1,0:T(8,128)}), f32[256,896]{1,0:T(8,128)}) %reduce-scatter.3.cloned.1.call-update) | async-done | bytes 917520 | tf_op jit(solution)/shard_map/reduce_scatter | solution.py:100
  304.5 2.0 multiply_reduce_fusion.4
  306.5 39.6 %all-reduce = (f32[]{:T(128)}, f32[]{:T(128)}) all-reduce(f32[]{:T(128)} %multiply_reduce_fusion.4, f32[]{:T(128)} %get-tuple-element.15), channel_id=1, replica_groups=mesh['dp'=8,'mp'=4] {'dp','mp'}, use_global_device_ids=true, to_apply=%region_15.16 | all-reduce | flops 2 | bytes 16 | tf_op jit(solution)/shard_map/psum | solution.py:109
  347.6 2.1 fusion.40
  349.7 67.0 %all-gather.8.cloned.1.call-done = bf16[2048,896]{1,0:T(8,128)(2,1)} async-done(((bf16[256,896]{1,0:T(8,128)(2,1)}), bf16[2048,896]{1,0:T(8,128)(2,1)}) %all-gather.8.cloned.1.call-update) | async-done | bytes 3670032 | tf_op jit(solution)/shard_map/all_gather | solution.py:79
  416.7 6.3 %multiply_reduce_fusion = (f32[512]{0:T(512)S(1)}, f32[512,896]{1,0:T(8,128)}) fusion(f32[512,896]{1,0:T(8,128)S(1)} %get-tuple-element.21, bf16[2048,896]{1,0:T(8,128)(2,1)} %all-gather.8.cloned.1.call-done, bf16[1,512,2048]{1,2,0:T(8,128)(2,1)} %all-gather.4.cloned.1.call-done), kind=kOutput, calls=%fused_computation.16 | convolution fusion | flops 1879965184 | bytes 9439232 | tf_op jit(solution)/shard_map/dot_general | solution.py:77
  423.0 5.8 psum.62
  428.8 3.1 fusion.10
  432.2 30.5 %all-reduce.6.cloned.1.call-done = f32[512,128]{1,0:T(8,128)} async-done(((f32[512,128]{1,0:T(8,128)}), f32[512,128]{1,0:T(8,128)}) %all-reduce.6.cloned.1.call-update) | async-done | bytes 262160 | tf_op jit(solution)/shard_map/psum | solution.py:82
  465.6 3.1 subtract_convert_fusion
  468.7 5.3 fusion
  474.1 132.8 %reduce-scatter.5.cloned.1.call-done = f32[256,896]{1,0:T(8,128)} async-done(((f32[2048,896]{1,0:T(8,128)}), f32[256,896]{1,0:T(8,128)}) %reduce-scatter.5.cloned.1.call-update) | async-done | bytes 917520 | tf_op jit(solution)/shard_map/reduce_scatter | solution.py:100
  606.9 2.3 divide_subtract_fusion
  (61 shorter events, 18.4 us)
Async XLA Ops:
  6.5 113.8 %copy-start = (bf16[896,128]{1,0:T(8,128)(2,1)S(1)}, bf16[896,128]{1,0:T(8,128)(2,1)}, u32[]{:S(2)}) copy-start(bf16[896,128]{1,0:T(8,128)(2,1)} %param.16) | copy-start | bytes 688132
  6.5 5.7 copy-start.9
  6.5 39.6 %all-gather.4.cloned.1.call-start = ((), (), s32[]{:S(2)}) async-start(), calls=%async_computation.2 | async-start | bytes 2621440 | tf_op jit(solution)/shard_map/all_gather | solution.py:50
  19.4 1.3 copy-start.4
  20.5 94.7 %all-gather.6.cloned.1.call-start = ((), (), s32[]{:S(2)}) async-start(), calls=%async_computation.3 | async-start | bytes 4128768 | tf_op jit(solution)/shard_map/all_gather | solution.py:79
  22.4 98.0 %copy-start.11 = (f32[896]{0:T(1024)S(1)}, f32[896]{0:T(1024)}, u32[]{:S(2)}) copy-start(f32[896]{0:T(1024)} %param.15) | copy-start | bytes 10756
  22.4 136.5 %all-reduce.8.cloned.1.call-start = ((), (), s32[]{:S(2)}) async-start(), calls=%async_computation.8 | async-start | bytes 1048576 | tf_op jit(solution)/shard_map/psum | solution.py:82
  115.2 6.9 %copy-start.3 = (bf16[2048,896]{1,0:T(8,128)(2,1)S(1)}, bf16[2048,896]{1,0:T(8,128)(2,1)}, u32[]{:S(2)}) copy-start(bf16[2048,896]{1,0:T(8,128)(2,1)} %param.14) | copy-start | bytes 11010052
  115.2 6.9 %copy-start.10 = (bf16[1,512,896]{2,1,0:T(8,128)(2,1)S(1)}, bf16[1,512,896]{2,1,0:T(8,128)(2,1)}, u32[]{:S(2)}) copy-start(bf16[1,512,896]{2,1,0:T(8,128)(2,1)} %param.13) | copy-start | bytes 2752516
  120.4 5.0 copy-start.1
  120.4 2.3 copy-start.6
  125.4 36.1 %copy-start.12 = (s32[1,512]{1,0:T(1,128)S(1)}, s32[1,512]{1,0:T(1,128)}, u32[]{:S(2)}) copy-start(s32[1,512]{1,0:T(1,128)} %param.19) | copy-start | bytes 6148
  127.1 177.4 %reduce-scatter.3.cloned.1.call-start = ((), (), s32[]{:S(2)}) async-start(), calls=%async_computation.4 | async-start | bytes 8257536 | tf_op jit(solution)/shard_map/reduce_scatter | solution.py:100
  163.1 3.2 copy-start.7
  171.7 245.0 %all-gather.8.cloned.1.call-start = ((), (), s32[]{:S(2)}) async-start(), calls=%async_computation.5 | async-start | bytes 4128768 | tf_op jit(solution)/shard_map/all_gather | solution.py:79
  349.7 113.1 %all-reduce.6.cloned.1.call-start = ((), (), s32[]{:S(2)}) async-start(), calls=%async_computation.6 | async-start | bytes 524288 | tf_op jit(solution)/shard_map/psum | solution.py:82
  423.0 39.8 %copy-start.2 = (f32[512,128]{1,0:T(8,128)S(1)}, f32[512,128]{1,0:T(8,128)}, u32[]{:S(2)}) copy-start(f32[512,128]{1,0:T(8,128)} %get-tuple-element.14) | copy-start | bytes 786436
  431.9 175.0 %reduce-scatter.5.cloned.1.call-start = ((), (), s32[]{:S(2)}) async-start(), calls=%async_computation.7 | async-start | bytes 8257536 | tf_op jit(solution)/shard_map/reduce_scatter | solution.py:100
  465.5 3.2 copy-start.8
  474.0 132.9 %copy-start.5 = (f32[256,896]{1,0:T(8,128)S(1)}, f32[256,896]{1,0:T(8,128)}, u32[]{:S(2)}) copy-start(f32[256,896]{1,0:T(8,128)} %reduce-scatter.3.cloned.1.call-done) | copy-start | bytes 2752516
Sparse Core Ops, SparseCore 0:
  20.6 25.5 all-gather.3
  48.4 66.7 all-gather.5
  127.2 31.6 all-reduce.7
  171.8 132.6 reduce-scatter.2
  349.8 66.8 all-gather.7
  432.0 30.6 all-reduce.5
  474.2 132.6 reduce-scatter.4
where the time goes:
time: 617 us; the launch traced here: 616 us
  waiting for transfers between devices  482 us (78%)
  blocking collectives  51.2 us (8%)
  matrix products  43.8 us (7%)
  other arithmetic  16.8 us (3%)
  between operations  15.1 us (2%)
  local copies, waits for them, and re-layouts  6.79 us (1%)
    reduce_scatter x2, waiting for transfers between devices, local(): lax.psum_scatter(lax.dot_general(attn, gdot, (((0,), (0,)), ((), ())), pr...  266 us
    all_gather x2, waiting for transfers between devices, local(): lax.all_gather(current.astype(jnp.bfloat16), 'dp', axis=0, tiled=True)  136 us
    psum x2, waiting for transfers between devices, local(): lax.psum((jnp.sum(h_loc * hdot, -1), jnp.dot(hdot * norm_gain, wide, prec...  56.4 us
    psum x1, blocking collectives, local(): product_sq = lax.psum(jnp.sum(hvp_rows * hvp_rows), ('dp', 'mp'))  39.6 us
    all_gather x1, waiting for transfers between devices, local(): attn = lax.all_gather(local_out[None], 'mp', axis=1, tiled=True)[0]  23.8 us
  transfers between devices with their start and end apart: 7, of which 7 were waited for; matrix products, arithmetic and copies ran while one was open for 0% of the time, Pallas kernels for 0%

commit v1 on v0

v1 whole, which is shorter than its diff:
```python
import functools

import jax
import jax.numpy as jnp
from jax import lax
from jax.experimental import pallas as pl
from jax.experimental.pallas import tpu as pltpu
from jax.sharding import PartitionSpec as P

D = 3584
HD = 256
HQ = 8
HK = 4
TAGS = 128
WINDOW = 256

DAMP = 0.01
NORM_EPS = 1e-06
MEAN_EPS = 1e-06

MESH = pl.DeviceIdType.MESH
VMEM_LIMIT = 48 * 1024 * 1024
CHUNKS = 2
F32 = jnp.float32
BF16 = jnp.bfloat16


def inner_of(size):
    return 1 << ((size.bit_length() - 1) // 2)


def remote(src, dst, send, recv, dp, mp):
    return pltpu.make_async_remote_copy(
        src_ref=src,
        dst_ref=dst,
        send_sem=send,
        recv_sem=recv,
        device_id=(dp, mp),
        device_id_type=MESH,
    )


def greet(peers):
    barrier = pltpu.get_barrier_semaphore()
    for dp, mp in peers:
        pl.semaphore_signal(barrier, inc=1, device_id=(dp, mp), device_id_type=MESH)
    pl.semaphore_wait(barrier, len(peers))


class Grid:
    def __init__(self, size):
        self.size = size
        self.inner = inner_of(size)
        self.outer = size // self.inner
        self.mp = lax.axis_index("mp")
        me = lax.axis_index("dp")
        self.z = me // self.inner
        self.x = me % self.inner

    def at(self, dz, dx):
        z = lax.rem(self.z + (dz + self.outer), self.outer)
        x = lax.rem(self.x + (dx + self.inner), self.inner)
        return z * self.inner + x

    def peers(self):
        out = [(self.at(dz, 0), self.mp) for dz in range(1, self.outer)]
        return out + [(self.at(0, dx), self.mp) for dx in range(1, self.inner)]


def part_rows(ref, device, rows, chunk):
    step = rows // CHUNKS
    return ref.at[pl.ds(pl.multiple_of(device * rows + chunk * step, step), step)]


def gather_start(grid, src, dst, local, send, recv):
    rows = src.shape[0]
    step = rows // CHUNKS
    me = grid.at(0, 0)
    sent = []
    for c in range(CHUNKS):
        piece = src.at[pl.ds(c * step, step)]
        place = part_rows(dst, me, rows, c)
        for dz in range(1, grid.outer):
            sent.append(remote(piece, place, send.at[dz, 0, c], recv.at[dz, 0, c], grid.at(dz, 0), grid.mp))
        for dx in range(1, grid.inner):
            sent.append(remote(piece, place, send.at[0, dx, c], recv.at[0, dx, c], grid.at(0, dx), grid.mp))
    for copy in sent:
        copy.start()
    own = pltpu.make_async_copy(src, dst.at[pl.ds(pl.multiple_of(me * rows, rows), rows)], local)
    own.start()
    return own, sent


def gather_finish(grid, src, dst, started, send, recv):
    rows = src.shape[0]
    own, sent = started
    for c in range(CHUNKS):
        for dz in range(1, grid.outer):
            place = part_rows(dst, grid.at(-dz, 0), rows, c)
            remote(place, place, send.at[dz, 0, c], recv.at[dz, 0, c], grid.at(dz, 0), grid.mp).wait_recv()
            for dx in range(1, grid.inner):
                copy = remote(place, place, send.at[dz, dx, c], recv.at[dz, dx, c], grid.at(0, dx), grid.mp)
                copy.start()
                sent.append(copy)
    for c in range(CHUNKS):
        for dz in range(grid.outer):
            for dx in range(1, grid.inner):
                place = part_rows(dst, grid.at(-dz, -dx), rows, c)
                remote(place, place, send.at[dz, dx, c], recv.at[dz, dx, c], grid.at(0, dx), grid.mp).wait_recv()
    own.wait()
    for copy in sent:
        copy.wait_send()


def first_kernel(size, starts, query, key, value, src, attn, gathered, mine, local, send, recv, send_m, recv_m):
    grid = Grid(size)
    q_rows, width = query.shape
    num_k = key.shape[0]
    ways = num_k // q_rows
    dp = lax.axis_index("dp")
    mp = grid.mp
    others = [lax.rem(mp + d, ways) for d in range(1, ways)]
    greet(grid.peers() + [(dp, other) for other in others])
    started = gather_start(grid, src, gathered, local.at[0], send, recv)

    q_pos = mp * q_rows + lax.broadcasted_iota(jnp.int32, (q_rows, num_k), 0)
    k_pos = lax.broadcasted_iota(jnp.int32, (q_rows, num_k), 1)
    q_file = jnp.zeros((q_rows, num_k), jnp.int32)
    k_file = jnp.zeros((q_rows, num_k), jnp.int32)
    for f in range(starts.shape[1]):
        q_file = q_file + (starts[0, f] <= q_pos).astype(jnp.int32)
        k_file = k_file + (starts[0, f] <= k_pos).astype(jnp.int32)
    allowed = (q_file == k_file) & (k_pos <= q_pos) & (q_pos - k_pos < WINDOW)
    for h in range(HQ):
        g = h // (HQ // HK)
        scores = lax.dot_general(
            query[:, h * HD : (h + 1) * HD],
            key[:, g * HD : (g + 1) * HD],
            (((1,), (1,)), ((), ())),
            preferred_element_type=F32,
        ) * (1.0 / HD**0.5)
        scores = 50.0 * jnp.tanh(scores / 50.0)
        expo = jnp.where(allowed, jnp.exp(scores), 0.0)
        weights = (expo / jnp.sum(expo, -1, keepdims=True)).astype(BF16)
        out = jnp.dot(weights, value[:, g * HD : (g + 1) * HD], preferred_element_type=F32)
        mine[:, h * HD : (h + 1) * HD] = out.astype(BF16)

    def rows_of(device):
        return attn.at[pl.ds(pl.multiple_of(device * q_rows, q_rows), q_rows)]

    sent = [
        remote(mine, rows_of(mp), send_m.at[d], recv_m.at[d], dp, other) for d, other in enumerate(others)
    ]
    for copy in sent:
        copy.start()
    own = pltpu.make_async_copy(mine, rows_of(mp), local.at[1])
    own.start()
    gather_finish(grid, src, gathered, started, send, recv)
    for d, other in enumerate(others):
        place = rows_of(lax.rem(mp + (ways - 1 - d), ways))
        remote(place, place, send_m.at[d], recv_m.at[d], dp, other).wait_recv()
    own.wait()
    for copy in sent:
        copy.wait_send()


def first(size, ways, starts, query, key, value, src):
    rows, cols = src.shape
    inner = inner_of(size)
    sems = pltpu.SemaphoreType.DMA((size // inner, inner, CHUNKS))
    vmem = pl.BlockSpec(memory_space=pltpu.VMEM)
    place = pl.BlockSpec(memory_space=pl.ANY)
    return pl.pallas_call(
        functools.partial(first_kernel, size),
        out_shape=(
            jax.ShapeDtypeStruct((key.shape[0], query.shape[1]), BF16),
            jax.ShapeDtypeStruct((rows * size, cols), BF16),
        ),
        in_specs=[pl.BlockSpec(memory_space=pltpu.SMEM), vmem, vmem, vmem, place],
        out_specs=(place, place),
        scratch_shapes=[
            pltpu.VMEM(query.shape, BF16),
            pltpu.SemaphoreType.DMA((2,)),
            sems,
            sems,
            pltpu.SemaphoreType.DMA((ways,)),
            pltpu.SemaphoreType.DMA((ways,)),
        ],
        compiler_params=pltpu.CompilerParams(
            collective_id=0, has_side_effects=True, vmem_limit_bytes=VMEM_LIMIT
        ),
        name="attend_and_gather",
    )(starts, query, key, value, src)


def curve_kernel(ways, early, *refs):
    if early:
        part, tags, packed, z_out, r_out, extra_out, got, mine, s1, r1, s2, r2 = refs
    else:
        part, tags, z_in, r_in, packed, extra_out, got, mine, s1, r1, s2, r2 = refs
    rows = part.shape[0] // ways
    dp = lax.axis_index("dp")
    mp = lax.axis_index("mp")
    others = [lax.rem(mp + d, ways) for d in range(1, ways)]
    greet([(dp, other) for other in others])

    def rows_of(device):
        return pl.ds(pl.multiple_of(device * rows, rows), rows)

    sent = [
        remote(part.at[rows_of(other)], got.at[d], s1.at[d], r1.at[d], dp, other)
        for d, other in enumerate(others)
    ]
    for copy in sent:
        copy.start()
    total = part[rows_of(mp), :].astype(F32)
    for d, copy in enumerate(sent):
        copy.wait_recv()
        total = total + got[d].astype(F32)
    if early:
        zval = total[:, :TAGS]
        zdot = total[:, TAGS : 2 * TAGS]
        extra = total[:, 2 * TAGS :]
        sumsq = extra[:, 2:3] + extra[:, 3:4]
        rscale = lax.rsqrt(sumsq / D + NORM_EPS)
        z_out[...] = zval
        r_out[...] = jnp.broadcast_to(rscale, r_out.shape)
    else:
        zdot = total[:, :TAGS]
        extra = total[:, TAGS:]
        zval = z_in[...]
        rscale = r_in[:, 0:1]
    along = extra[:, 0:1] + extra[:, 1:2]
    extra_out[...] = extra[:8, :]
    tanh_val = jnp.tanh(rscale * zval / 30.0)
    slope = 1.0 - tanh_val * tanh_val
    expo = jnp.exp(30.0 * tanh_val)
    probs = expo / jnp.sum(expo, -1, keepdims=True)
    lane = lax.broadcasted_iota(jnp.int32, zval.shape, 1)
    onehot = (tags[rows_of(mp), :] == lane).astype(F32)
    dlogit = probs - onehot
    wgrad = dlogit * slope
    rho = jnp.sum(wgrad * zval, -1, keepdims=True)
    cube = rscale * rscale * rscale / D
    rdot = -cube * along
    mdot = rdot * zval + rscale * zdot
    ldot = slope * mdot
    pdot = probs * (ldot - jnp.sum(probs * ldot, -1, keepdims=True))
    wdot = pdot * slope - dlogit * 2.0 * tanh_val * slope * mdot / 30.0
    rhodot = jnp.sum(wdot * zval + wgrad * zdot, -1, keepdims=True)
    mixed = rdot * wgrad + rscale * wdot
    coeff = rhodot * cube + 3.0 * rho * rscale * rscale * rdot / D
    pull = rho * cube
    coeff_high = coeff.astype(BF16).astype(F32)
    pull_high = pull.astype(BF16).astype(F32)
    columns = jnp.where(lane == 0, coeff_high, 0.0)
    columns = jnp.where(lane == 1, coeff - coeff_high, columns)
    columns = jnp.where(lane == 2, pull_high, columns)
    columns = jnp.where(lane == 3, pull - pull_high, columns)
    mine[:, :TAGS] = mixed.astype(BF16)
    mine[:, TAGS:] = columns.astype(BF16)
    back = [
        remote(mine, packed.at[rows_of(mp)], s2.at[d], r2.at[d], dp, other)
        for d, other in enumerate(others)
    ]
    for copy in back:
        copy.start()
    packed[rows_of(mp), :] = mine[...]
    for d, other in enumerate(others):
        place = packed.at[rows_of(lax.rem(mp + (ways - 1 - d), ways))]
        remote(place, place, s2.at[d], r2.at[d], dp, other).wait_recv()
    for copy in sent + back:
        copy.wait_send()


def curve(ways, part, tags, state, collective_id):
    early = state is None
    tokens, width = part.shape
    rows = tokens // ways
    vmem = pl.BlockSpec(memory_space=pltpu.VMEM)
    operands = (part, tags) if early else (part, tags) + state
    out_shape = [jax.ShapeDtypeStruct((tokens, 2 * TAGS), BF16)]
    if early:
        out_shape += [jax.ShapeDtypeStruct((rows, TAGS), F32)] * 2
    out_shape += [jax.ShapeDtypeStruct((8, TAGS), F32)]
    sems = pltpu.SemaphoreType.DMA((ways,))
    return pl.pallas_call(
        functools.partial(curve_kernel, ways, early),
        out_shape=tuple(out_shape),
        in_specs=[vmem] * len(operands),
        out_specs=(vmem,) * len(out_shape),
        scratch_shapes=[
            pltpu.VMEM((ways - 1, rows, width), BF16),
            pltpu.VMEM((rows, 2 * TAGS), BF16),
            sems,
            sems,
            sems,
            sems,
        ],
        compiler_params=pltpu.CompilerParams(
            collective_id=collective_id, has_side_effects=True, vmem_limit_bytes=VMEM_LIMIT
        ),
        name="curve_early" if early else "curve_late",
    )(*operands)


def reduce_rows(grid, src, own, from_x, pair, from_z, send, recv):
    rows = own.shape[0]
    step = rows // CHUNKS
    sent = []

    def piece(ref, c):
        return ref.at[pl.ds(c * step, step)]

    order = list(range(1, grid.outer)) + [0]
    for dz in order:
        for c in range(CHUNKS):
            for dx in range(1, grid.inner):
                copy = remote(
                    part_rows(src, grid.at(dz, dx), rows, c),
                    piece(from_x.at[dz, dx - 1], c),
                    send.at[dz, dx, c],
                    recv.at[dz, dx, c],
                    grid.at(0, dx),
                    grid.mp,
                )
                copy.start()
                sent.append(copy)

    def paired(dz, c):
        total = part_rows(src, grid.at(dz, 0), rows, c)[...].astype(F32)
        for dx in range(1, grid.inner):
            place = piece(from_x.at[dz, dx - 1], c)
            remote(place, place, send.at[dz, dx, c], recv.at[dz, dx, c], grid.at(0, dx), grid.mp).wait_recv()
            total = total + place[...].astype(F32)
        return total

    for dz in range(1, grid.outer):
        for c in range(CHUNKS):
            place = piece(pair.at[dz - 1], c)
            place[...] = paired(dz, c).astype(BF16)
            copy = remote(
                place,
                piece(from_z.at[dz - 1], c),
                send.at[dz, 0, c],
                recv.at[dz, 0, c],
                grid.at(dz, 0),
                grid.mp,
            )
            copy.start()
            sent.append(copy)
    for c in range(CHUNKS):
        total = paired(0, c)
        for dz in range(1, grid.outer):
            place = piece(from_z.at[dz - 1], c)
            remote(place, place, send.at[dz, 0, c], recv.at[dz, 0, c], grid.at(dz, 0), grid.mp).wait_recv()
            total = total + place[...].astype(F32)
        piece(own, c)[...] = total
    return sent


def reduce_scratch(size, rows, cols):
    inner = inner_of(size)
    outer = size // inner
    sems = pltpu.SemaphoreType.DMA((outer, inner, CHUNKS))
    return [
        pltpu.VMEM((outer, inner - 1, rows, cols), BF16),
        pltpu.VMEM((outer - 1, rows, cols), BF16),
        pltpu.VMEM((outer - 1, rows, cols), BF16),
        sems,
        sems,
    ]


def sum_gather_kernel(size, src, own, gathered, from_x, pair, from_z, s1, r1, mine, local, s2, r2):
    grid = Grid(size)
    greet(grid.peers())
    sent = reduce_rows(grid, src, own, from_x, pair, from_z, s1, r1)
    mine[...] = own[...].astype(BF16)
    started = gather_start(grid, mine, gathered, local.at[0], s2, r2)
    gather_finish(grid, mine, gathered, started, s2, r2)
    for copy in sent:
        copy.wait_send()


def sum_gather(size, src):
    total, cols = src.shape
    rows = total // size
    inner = inner_of(size)
    sems = pltpu.SemaphoreType.DMA((size // inner, inner, CHUNKS))
    vmem = pl.BlockSpec(memory_space=pltpu.VMEM)
    return pl.pallas_call(
        functools.partial(sum_gather_kernel, size),
        out_shape=(
            jax.ShapeDtypeStruct((rows, cols), F32),
            jax.ShapeDtypeStruct((total, cols), BF16),
        ),
        in_specs=[vmem],
        out_specs=(vmem, pl.BlockSpec(memory_space=pl.ANY)),
        scratch_shapes=reduce_scratch(size, rows, cols)
        + [pltpu.VMEM((rows, cols), BF16), pltpu.SemaphoreType.DMA((1,)), sems, sems],
        compiler_params=pltpu.CompilerParams(
            collective_id=2, has_side_effects=True, vmem_limit_bytes=VMEM_LIMIT
        ),
        name="sum_and_gather",
    )(src)


def sum_kernel(size, src, scalars, own, scalar_sum, from_x, pair, from_z, s1, r1, got, s2, r2):
    grid = Grid(size)
    others = [lax.rem(lax.axis_index("dp") + d, size) for d in range(1, size)]
    greet([(other, grid.mp) for other in others])
    small = [
        remote(scalars, got.at[d], s2.at[d], r2.at[d], other, grid.mp) for d, other in enumerate(others)
    ]
    for copy in small:
        copy.start()
    sent = reduce_rows(grid, src, own, from_x, pair, from_z, s1, r1)
    total = scalars[...]
    for d, copy in enumerate(small):
        copy.wait_recv()
        total = total + got[d]
    scalar_sum[...] = total
    for copy in sent + small:
        copy.wait_send()


def sum_only(size, src, scalars):
    total, cols = src.shape
    rows = total // size
    vmem = pl.BlockSpec(memory_space=pltpu.VMEM)
    return pl.pallas_call(
        functools.partial(sum_kernel, size),
        out_shape=(
            jax.ShapeDtypeStruct((rows, cols), F32),
            jax.ShapeDtypeStruct(scalars.shape, F32),
        ),
        in_specs=[vmem, vmem],
        out_specs=(vmem, vmem),
        scratch_shapes=reduce_scratch(size, rows, cols)
        + [
            pltpu.VMEM((size - 1,) + scalars.shape, F32),
            pltpu.SemaphoreType.DMA((size - 1,)),
            pltpu.SemaphoreType.DMA((size - 1,)),
        ],
        compiler_params=pltpu.CompilerParams(
            collective_id=4, has_side_effects=True, vmem_limit_bytes=VMEM_LIMIT
        ),
        name="sum_rows",
    )(src, scalars)


def split_columns(values, tokens):
    out = []
    for value in values:
        value = jnp.broadcast_to(value, (tokens,))
        high = lax.reduce_precision(value, 8, 7)
        out += [high, value - high]
    block = jnp.stack(out, -1).astype(BF16)
    return jnp.pad(block, ((0, 0), (0, TAGS - len(out))))


def local(size, ways, queries, keys, values, stream, out_proj, norm_gain, tag_proj, direction, starts, tags):
    count = HQ * HD * D
    tokens = keys.shape[1]
    tag_column = tags[0][:, None]
    attn, rounded = first(
        size, ways, starts, queries[0], keys[0], values[0], direction.astype(BF16)
    )
    h_loc = stream[0].astype(F32) + jnp.dot(attn, out_proj, preferred_element_type=F32)

    def scores(value):
        return jnp.dot((value * norm_gain).astype(BF16), tag_proj, preferred_element_type=F32).astype(BF16)

    def product(packed, hdot):
        mixed = packed[:, :TAGS]
        columns = packed[:, TAGS : TAGS + 4].astype(F32)
        coeff = columns[:, 0:1] + columns[:, 1:2]
        pull = columns[:, 2:3] + columns[:, 3:4]
        back = lax.dot_general(mixed, tag_proj, (((1,), (1,)), ((), ())), preferred_element_type=F32)
        gdot = (back * norm_gain - coeff * h_loc - pull * hdot).astype(BF16)
        return lax.dot_general(attn, gdot, (((0,), (0,)), ((), ())), preferred_element_type=F32).astype(BF16)

    hdot = jnp.dot(attn, rounded, preferred_element_type=F32)
    extra = split_columns([jnp.sum(h_loc * hdot, -1), jnp.sum(h_loc * h_loc, -1)], tokens)
    part = jnp.concatenate([scores(h_loc), scores(hdot), extra], 1)
    packed, zval, rscale, _ = curve(ways, part, tag_column, None, 1)
    once, once_all = sum_gather(size, product(packed, hdot))

    hdot = jnp.dot(attn, once_all, preferred_element_type=F32)
    extra = split_columns(
        [jnp.sum(h_loc * hdot, -1), jnp.sum(direction * direction), jnp.sum(once * once)], tokens
    )
    part = jnp.concatenate([scores(hdot), extra], 1)
    packed, scalars = curve(ways, part, tag_column, (zval, rscale), 3)
    twice, sums = sum_only(size, product(packed, hdot), scalars)

    early_norm = sums[0, 2] + sums[0, 3]
    product_sq = sums[0, 4] + sums[0, 5]
    sigma = 2.0 * jnp.sqrt((product_sq / count + MEAN_EPS) / (early_norm / count + MEAN_EPS))
    keep = 1.0 - DAMP
    return (
        (1.0 + keep * (1.0 + keep)) * direction
        - ((1.0 + 2.0 * keep) / sigma) * once
        + twice / sigma / sigma
    )


def solution(mesh):
    return jax.shard_map(
        functools.partial(local, mesh.shape["dp"], mesh.shape["mp"]),
        mesh=mesh,
        in_specs=(
            P("dp", "mp", None),
            P("dp", None, None),
            P("dp", None, None),
            P("dp", None, "mp"),
            P(None, "mp"),
            P("mp"),
            P("mp", None),
            P("dp", "mp"),
            P("dp", None),
            P("dp", None),
        ),
        out_specs=P("dp", "mp"),
        check_vma=False,
    )
```

time: 617 us -> 298 us (0.48)
  waiting for transfers between devices: 482 us -> 0 us
  Pallas kernels: 0 us -> 242 us
  blocking collectives: 51.2 us -> 0 us
  matrix products: 43.8 us -> 30.7 us
  other arithmetic: 16.8 us -> 5.37 us
    reduce_scatter x2 -> x0, waiting for transfers between devices: 266 us -> none  [local(): lax.psum_scatter(lax.dot_general(attn, gdot, (((0,), (0,)), ((), ())), pr...]
    pallas_call x0 -> x5, Pallas kernels: none -> 242 us  [the longest x1 104 us: sum_gather(): pl.pallas_call(functools.partial(sum_gather_kernel, size), out_shape=(jax...]
    all_gather x3 -> x0, waiting for transfers between devices: 160 us -> none  [the longest x2 136 us: local(): lax.all_gather(current.astype(jnp.bfloat16), 'dp', axis=0, tiled=True)]
    psum x2 -> x0, waiting for transfers between devices: 56.4 us -> none  [local(): lax.psum((jnp.sum(h_loc * hdot, -1), jnp.dot(hdot * norm_gain, wide, prec...]
    psum x3 -> x0, blocking collectives: 51.2 us -> none  [the longest x1 39.6 us: local(): product_sq = lax.psum(jnp.sum(hvp_rows * hvp_rows), ('dp', 'mp'))]
    dot_general x12 -> x8, matrix products: 43.8 us -> 30.7 us  [the longest x2 14 us: product(): lax.dot_general(attn, gdot, (((0,), (0,)), ((), ())), preferred_element_t...]
    reduce_sum x9 -> x2, other arithmetic: 12.2 us -> 3.23 us  [the longest x1 2.4 us: local(): jnp.sum(direction * direction)]
    unnamed x26 -> x32, local copies, waits for them, and re-layouts: 0.92 us -> 8.48 us
  transfers between devices with their start and end apart: 7 -> 0, of which waited for: 7 -> 0; matrix products, arithmetic and copies ran while one was open for 0% -> 0% of each run, Pallas kernels for 0% -> 0%
where the time goes in v1:
time: 298 us; the launch traced here: 297 us
  Pallas kernels  242 us (81%)
  matrix products  30.7 us (10%)
  local copies, waits for them, and re-layouts  9.67 us (3%)
  between operations  9.25 us (3%)
  other arithmetic  5.37 us (2%)
    pallas_call x1, Pallas kernels, sum_gather(): pl.pallas_call(functools.partial(sum_gather_kernel, size), out_shape=(jax...  104 us
    pallas_call x1, Pallas kernels, sum_only(): pl.pallas_call(functools.partial(sum_kernel, size), out_shape=(jax.ShapeD...  62.8 us
    pallas_call x1, Pallas kernels, first(): pl.pallas_call(functools.partial(first_kernel, size), out_shape=(jax.Shap...  54.3 us
    pallas_call x2, Pallas kernels, curve(): pl.pallas_call(functools.partial(curve_kernel, ways, early), out_shape=tu...  21.3 us
    dot_general x2, matrix products, product(): lax.dot_general(attn, gdot, (((0,), (0,)), ((), ())), preferred_element_t...  14 us
    unnamed x32, local copies, waits for them, and re-layouts  8.48 us
    dot_general x1, matrix products, local(): hdot = jnp.dot(attn, once_all, preferred_element_type=F32)  6.31 us

profile of v1, /device:TPU:0, one launch (start us, length us, event | category | flops | bytes accessed | tf_op | source)
XLA Modules:
  0.0 297.0 jit_solution(9355861925497476970)
XLA Ops:
  0.0 2.4 multiply_reduce_fusion.4
  2.4 1.2 copy-done.3
  3.6 1.0 copy-done.4
  4.7 0.7 copy-done.5
  5.3 54.3 %attend_and_gather.1 = (bf16[512,2048]{1,0:T(8,128)(2,1)S(1)}, bf16[2048,896]{1,0:T(8,128)(2,1)}) custom-call(s32[1,4]{1,0:T(1,128)S(1)} %copy-done.5, bf16[128,2048]{1,0:T(8,128)(2,1)S(1)} %bitcast.27, bf16[512,1024]{1,0:T(8,128)(2,1)S(1)} %bitcast.25, bf16[512,1024]{1,0:T(8,128)(2,1)S(1)} %bitcast.26, bf16[256,896]{1,0:T(8,128)(2,1)S(1)} %get-tuple-element.34.src), custom_call_target="tpu_custom_call" | custom-call | tf_op jit(solution)/shard_map/attend_and_gather/pallas_call | solution.py:173
  59.6 5.2 %fusion.25 = f32[512,896]{1,0:T(8,128)S(1)} fusion(bf16[512,2048]{1,0:T(8,128)(2,1)S(1)} %get-tuple-element.16, bf16[2048,896]{1,0:T(8,128)(2,1)} %get-tuple-element.17), kind=kOutput, calls=%fused_computation.55 | convolution fusion | flops 1879048192 | bytes 7602176 | tf_op jit(solution)/shard_map/dot_general | solution.py:484
  64.8 2.5 multiply_reduce_fusion.2
  67.7 0.4 convolution_convert_fusion.4
  68.1 1.5 copy-done.11
  70.4 11.4 %curve_early.1 = (bf16[512,256]{1,0:T(8,128)(2,1)S(1)}, f32[128,128]{1,0:T(8,128)S(1)}, f32[128,128]{1,0:T(8,128)S(1)}, f32[8,128]{1,0:T(8,128)}) custom-call(bf16[512,384]{1,0:T(8,128)(2,1)S(1)} %fusion.11.refs_0_, s32[512,1]{1,0:T(8,128)S(1)} %copy.28.refs_1_), custom_call_target="tpu_custom_call" | custom-call | tf_op jit(solution)/shard_map/curve_early/pallas_call | solution.py:287
  81.8 0.4 fusion.16
  82.3 6.7 %convolution_convert_fusion.1.src = bf16[2048,896]{1,0:T(8,128)(2,1)} fusion(bf16[512,2048]{1,0:T(8,128)(2,1)} %copy-done.7, f32[512,896]{1,0:T(8,128)} %copy-done.10, f32[512,896]{1,0:T(8,128)S(1)} %get-tuple-element.45, bf16[896,128]{1,0:T(8,128)(2,1)S(1)} %copy-done, f32[512]{0:T(512)S(1)} %get-tuple-element.32, f32[512]{0:T(512)S(1)} %get-tuple-element.31, ...), kind=kOutput, calls=%fused_computation.1 | convolution fusion | flops 2001076224 | bytes 9805824 | tf_op jit(solution)/shard_map/dot_general | solution.py:482
  89.0 103.7 %sum_and_gather.1 = (f32[256,896]{1,0:T(8,128)S(1)}, bf16[2048,896]{1,0:T(8,128)(2,1)S(1)}) custom-call(bf16[2048,896]{1,0:T(8,128)(2,1)} %convolution_convert_fusion.1.src), custom_call_target="tpu_custom_call" | custom-call | tf_op jit(solution)/shard_map/sum_and_gather/pallas_call | solution.py:392
  192.7 1.8 copy-done.6
  194.4 0.8 multiply_reduce_fusion.3
  197.8 6.3 %multiply_reduce_fusion = (f32[512]{0:T(512)S(1)}, f32[512,896]{1,0:T(8,128)}) fusion(f32[512,896]{1,0:T(8,128)S(1)} %get-tuple-element.45, bf16[512,2048]{1,0:T(8,128)(2,1)} %copy-done.7, bf16[2048,896]{1,0:T(8,128)(2,1)} %copy-done.6), kind=kOutput, calls=%fused_computation.4 | convolution fusion | flops 1879965184 | bytes 9439232 | tf_op jit(solution)/shard_map/dot_general | solution.py:490
  208.2 1.9 convolution_convert_fusion.2
  210.2 9.9 %curve_late.1 = (bf16[512,256]{1,0:T(8,128)(2,1)S(1)}, f32[8,128]{1,0:T(8,128)S(1)}) custom-call(bf16[512,256]{1,0:T(8,128)(2,1)S(1)} %fusion.12.refs_0_, s32[512,1]{1,0:T(8,128)S(1)} %copy.28.refs_1_, f32[128,128]{1,0:T(8,128)S(1)} %get-tuple-element.21.refs_2_, f32[128,128]{1,0:T(8,128)S(1)} %get-tuple-element.22.refs_3_), custom_call_target="tpu_custom_call" | custom-call | tf_op jit(solution)/shard_map/curve_late/pallas_call | solution.py:287
  220.1 0.4 fusion.14
  220.5 7.3 %convolution_convert_fusion.src = bf16[2048,896]{1,0:T(8,128)(2,1)} fusion(bf16[512,2048]{1,0:T(8,128)(2,1)} %copy-done.7, f32[512,896]{1,0:T(8,128)} %get-tuple-element.47, f32[512,896]{1,0:T(8,128)} %copy-done.9, bf16[896,128]{1,0:T(8,128)(2,1)S(1)} %copy-done, f32[512]{0:T(512)S(1)} %get-tuple-element.30, f32[512]{0:T(512)S(1)} %get-tuple-element.29, ...), kind=kOutput, calls=%fused_computation | convolution fusion | flops 2001076224 | bytes 9805824 | tf_op jit(solution)/shard_map/dot_general | solution.py:482
  227.8 2.0 copy-done.1
  229.9 62.8 %sum_rows.1 = (f32[256,896]{1,0:T(8,128)S(1)}, f32[8,128]{1,0:T(8,128)S(1)}) custom-call(bf16[2048,896]{1,0:T(8,128)(2,1)S(1)} %copy-done.1, f32[8,128]{1,0:T(8,128)S(1)} %get-tuple-element.24.scalars), custom_call_target="tpu_custom_call" | custom-call | tf_op jit(solution)/shard_map/sum_rows/pallas_call | solution.py:432
  292.6 0.6 fusion.24
  295.9 1.1 divide_add_fusion
  (42 shorter events, 1.4 us)
Async XLA Ops:
  0.0 67.6 %copy-start = (bf16[896,128]{1,0:T(8,128)(2,1)S(1)}, bf16[896,128]{1,0:T(8,128)(2,1)}, u32[]{:S(2)}) copy-start(bf16[896,128]{1,0:T(8,128)(2,1)} %param.16) | copy-start | bytes 688132
  0.0 2.4 copy-start.2
  2.4 1.2 copy-start.3
  3.6 1.0 copy-start.4
  4.7 0.7 copy-start.5
  59.6 5.2 %copy-start.7 = (bf16[512,2048]{1,0:T(8,128)(2,1)}, bf16[512,2048]{1,0:T(8,128)(2,1)S(1)}, u32[]{:S(2)}) copy-start(bf16[512,2048]{1,0:T(8,128)(2,1)S(1)} %get-tuple-element.16) | copy-start | bytes 6291460
  59.6 5.2 %copy-start.14 = (bf16[2048,896]{1,0:T(8,128)(2,1)S(1)}, bf16[2048,896]{1,0:T(8,128)(2,1)}, u32[]{:S(2)}) copy-start(bf16[2048,896]{1,0:T(8,128)(2,1)} %param.14) | copy-start | bytes 11010052
  59.6 5.2 %copy-start.15 = (bf16[1,512,896]{2,1,0:T(8,128)(2,1)S(1)}, bf16[1,512,896]{2,1,0:T(8,128)(2,1)}, u32[]{:S(2)}) copy-start(bf16[1,512,896]{2,1,0:T(8,128)(2,1)} %param.13) | copy-start | bytes 2752516
  64.8 2.6 copy-start.10
  64.8 2.8 copy-start.12
  67.4 130.4 %copy-start.9 = (f32[512,896]{1,0:T(8,128)}, f32[512,896]{1,0:T(8,128)S(1)}, u32[]{:S(2)}) copy-start(f32[512,896]{1,0:T(8,128)S(1)} %get-tuple-element.45) | copy-start | bytes 5505028
  67.6 1.9 copy-start.11
  69.6 0.7 copy-start.13
  192.7 1.8 copy-start.6
  227.8 2.0 copy-start.1
  229.9 66.1 %copy-start.8 = (f32[256,896]{1,0:T(8,128)S(1)}, f32[256,896]{1,0:T(8,128)}, u32[]{:S(2)}) copy-start(f32[256,896]{1,0:T(8,128)} %param.17) | copy-start | bytes 2752516

commit v2 on v1

--- a/solution.py
+++ b/solution.py
@@ -21,6 +21,7 @@
 MESH = pl.DeviceIdType.MESH
 VMEM_LIMIT = 48 * 1024 * 1024
 CHUNKS = 2
+AHEAD = 2
 F32 = jnp.float32
 BF16 = jnp.bfloat16
 
@@ -72,47 +73,113 @@
     return ref.at[pl.ds(pl.multiple_of(device * rows + chunk * step, step), step)]
 
 
-def gather_start(grid, src, dst, local, send, recv):
-    rows = src.shape[0]
-    step = rows // CHUNKS
-    me = grid.at(0, 0)
-    sent = []
-    for c in range(CHUNKS):
-        piece = src.at[pl.ds(c * step, step)]
-        place = part_rows(dst, me, rows, c)
-        for dz in range(1, grid.outer):
-            sent.append(remote(piece, place, send.at[dz, 0, c], recv.at[dz, 0, c], grid.at(dz, 0), grid.mp))
-        for dx in range(1, grid.inner):
-            sent.append(remote(piece, place, send.at[0, dx, c], recv.at[0, dx, c], grid.at(0, dx), grid.mp))
-    for copy in sent:
-        copy.start()
-    own = pltpu.make_async_copy(src, dst.at[pl.ds(pl.multiple_of(me * rows, rows), rows)], local)
-    own.start()
-    return own, sent
-
-
-def gather_finish(grid, src, dst, started, send, recv):
-    rows = src.shape[0]
-    own, sent = started
-    for c in range(CHUNKS):
-        for dz in range(1, grid.outer):
-            place = part_rows(dst, grid.at(-dz, 0), rows, c)
-            remote(place, place, send.at[dz, 0, c], recv.at[dz, 0, c], grid.at(dz, 0), grid.mp).wait_recv()
-            for dx in range(1, grid.inner):
-                copy = remote(place, place, send.at[dz, dx, c], recv.at[dz, dx, c], grid.at(0, dx), grid.mp)
-                copy.start()
-                sent.append(copy)
-    for c in range(CHUNKS):
-        for dz in range(grid.outer):
-            for dx in range(1, grid.inner):
-                place = part_rows(dst, grid.at(-dz, -dx), rows, c)
-                remote(place, place, send.at[dz, dx, c], recv.at[dz, dx, c], grid.at(0, dx), grid.mp).wait_recv()
-    own.wait()
-    for copy in sent:
-        copy.wait_send()
-
-
-def first_kernel(size, starts, query, key, value, src, attn, gathered, mine, local, send, recv, send_m, recv_m):
+class Gather:
+    def __init__(self, grid, src, dst, local, send, recv, send_x, recv_x):
+        self.grid = grid
+        self.src = src
+        self.dst = dst
+        self.local = local
+        self.line = (send, recv)
+        self.side = (send_x, recv_x)
+        self.rows = src.shape[0]
+
+    def block(self, way, hops, dx, c):
+        z = self.grid.z - hops * way
+        x = lax.rem(self.grid.x + (dx + self.grid.inner), self.grid.inner)
+        return part_rows(self.dst, z * self.grid.inner + x, self.rows, c)
+
+    def arrives(self, way, hops):
+        return self.grid.z >= hops if way > 0 else self.grid.z + hops < self.grid.outer
+
+    def goes_on(self, way):
+        return self.grid.z < self.grid.outer - 1 if way > 0 else self.grid.z > 0
+
+    def hop(self, piece, way, hops, c):
+        send, recv = self.line
+        lane = (way + 1) // 2
+        dp = (self.grid.z + way) * self.grid.inner + self.grid.x
+        return remote(
+            piece, self.block(way, hops, 0, c), send.at[lane, hops, c], recv.at[lane, hops + 1, c], dp, self.grid.mp
+        )
+
+    def aside(self, piece, way, hops, dx, c):
+        send, recv = self.side
+        lane = (way + 1) // 2
+        return remote(
+            piece,
+            self.block(way, hops, 0, c),
+            send.at[lane, hops, dx, c],
+            recv.at[lane, hops, dx, c],
+            self.grid.at(0, dx),
+            self.grid.mp,
+        )
+
+    def own(self, c):
+        step = self.rows // CHUNKS
+        return self.src.at[pl.ds(c * step, step)]
+
+    def start(self):
+        for c in range(CHUNKS):
+            for way in (1, -1):
+                pl.when(self.goes_on(way))(lambda way=way, c=c: self.hop(self.own(c), way, 0, c).start())
+            for dx in range(1, self.grid.inner):
+                self.aside(self.own(c), 1, 0, dx, c).start()
+        me = self.grid.at(0, 0)
+        whole = self.dst.at[pl.ds(pl.multiple_of(me * self.rows, self.rows), self.rows)]
+        self.kept = pltpu.make_async_copy(self.src, whole, self.local)
+        self.kept.start()
+
+    def take(self, way, hops, c):
+        piece = self.block(way, hops, 0, c)
+        lane = (way + 1) // 2
+        send, recv = self.line
+        dp = (self.grid.z - way) * self.grid.inner + self.grid.x
+        remote(piece, piece, send.at[lane, hops, c], recv.at[lane, hops, c], dp, self.grid.mp).wait_recv()
+        if hops < self.grid.outer - 1:
+            pl.when(self.goes_on(way))(lambda: self.hop(piece, way, hops, c).start())
+        for dx in range(1, self.grid.inner):
+            self.aside(piece, way, hops, dx, c).start()
+
+    def take_aside(self, way, hops, c):
+        for dx in range(1, self.grid.inner):
+            piece = self.block(way, hops, -dx, c)
+            self.aside(piece, way, hops, dx, c).wait_recv()
+
+    def settle(self, way, hops, c):
+        piece = self.own(c) if hops == 0 else self.block(way, hops, 0, c)
+        if hops < self.grid.outer - 1:
+            pl.when(self.goes_on(way))(lambda: self.hop(piece, way, hops, c).wait_send())
+        if hops or way > 0:
+            for dx in range(1, self.grid.inner):
+                self.aside(piece, way, hops, dx, c).wait_send()
+
+    def finish(self):
+        outer = self.grid.outer
+        for act in (self.take, self.take_aside, self.settle):
+            for hops in range(outer):
+                if hops == 0 and act == self.take:
+                    continue
+                for c in range(CHUNKS):
+                    for way in (1, -1):
+                        if hops == 0:
+                            if act == self.settle or way > 0:
+                                act(way, hops, c)
+                        else:
+                            pl.when(self.arrives(way, hops))(
+                                lambda act=act, way=way, hops=hops, c=c: act(way, hops, c)
+                            )
+        self.kept.wait()
+
+
+def gather_scratch(size):
+    inner = inner_of(size)
+    outer = size // inner
+    line = pltpu.SemaphoreType.DMA((2, outer, CHUNKS))
+    side = pltpu.SemaphoreType.DMA((2, outer, inner, CHUNKS))
+    return [line, line, side, side]
+
+
+def first_kernel(size, starts, query, key, value, src, attn, gathered, mine, local, send_m, recv_m, *sems):
     grid = Grid(size)
     q_rows, width = query.shape
     num_k = key.shape[0]
@@ -121,7 +188,8 @@
     mp = grid.mp
     others = [lax.rem(mp + d, ways) for d in range(1, ways)]
     greet(grid.peers() + [(dp, other) for other in others])
-    started = gather_start(grid, src, gathered, local.at[0], send, recv)
+    gather = Gather(grid, src, gathered, local.at[0], *sems)
+    gather.start()
 
     q_pos = mp * q_rows + lax.broadcasted_iota(jnp.int32, (q_rows, num_k), 0)
     k_pos = lax.broadcasted_iota(jnp.int32, (q_rows, num_k), 1)
@@ -155,7 +223,7 @@
         copy.start()
     own = pltpu.make_async_copy(mine, rows_of(mp), local.at[1])
     own.start()
-    gather_finish(grid, src, gathered, started, send, recv)
+    gather.finish()
     for d, other in enumerate(others):
         place = rows_of(lax.rem(mp + (ways - 1 - d), ways))
         remote(place, place, send_m.at[d], recv_m.at[d], dp, other).wait_recv()
@@ -166,8 +234,6 @@
 
 def first(size, ways, starts, query, key, value, src):
     rows, cols = src.shape
-    inner = inner_of(size)
-    sems = pltpu.SemaphoreType.DMA((size // inner, inner, CHUNKS))
     vmem = pl.BlockSpec(memory_space=pltpu.VMEM)
     place = pl.BlockSpec(memory_space=pl.ANY)
     return pl.pallas_call(
@@ -181,11 +247,10 @@
         scratch_shapes=[
             pltpu.VMEM(query.shape, BF16),
             pltpu.SemaphoreType.DMA((2,)),
-            sems,
-            sems,
             pltpu.SemaphoreType.DMA((ways,)),
             pltpu.SemaphoreType.DMA((ways,)),
-        ],
+        ]
+        + gather_scratch(size),
         compiler_params=pltpu.CompilerParams(
             collective_id=0, has_side_effects=True, vmem_limit_bytes=VMEM_LIMIT
         ),
@@ -312,9 +377,12 @@
     def piece(ref, c):
         return ref.at[pl.ds(c * step, step)]
 
-    order = list(range(1, grid.outer)) + [0]
-    for dz in order:
-        for c in range(CHUNKS):
+    order = [(dz, c) for dz in list(range(1, grid.outer)) + [0] for c in range(CHUNKS)]
+    queue = list(order)
+
+    def feed():
+        if queue:
+            dz, c = queue.pop(0)
             for dx in range(1, grid.inner):
                 copy = remote(
                     part_rows(src, grid.at(dz, dx), rows, c),
@@ -327,28 +395,34 @@
                 copy.start()
                 sent.append(copy)
 
+    for _ in range(AHEAD):
+        feed()
+
     def paired(dz, c):
         total = part_rows(src, grid.at(dz, 0), rows, c)[...].astype(F32)
         for dx in range(1, grid.inner):
             place = piece(from_x.at[dz, dx - 1], c)
             remote(place, place, send.at[dz, dx, c], recv.at[dz, dx, c], grid.at(0, dx), grid.mp).wait_recv()
+            if dx == grid.inner - 1:
+                feed()
             total = total + place[...].astype(F32)
         return total
 
-    for dz in range(1, grid.outer):
-        for c in range(CHUNKS):
-            place = piece(pair.at[dz - 1], c)
-            place[...] = paired(dz, c).astype(BF16)
-            copy = remote(
-                place,
-                piece(from_z.at[dz - 1], c),
-                send.at[dz, 0, c],
-                recv.at[dz, 0, c],
-                grid.at(dz, 0),
-                grid.mp,
-            )
-            copy.start()
-            sent.append(copy)
+    for dz, c in order:
+        if dz == 0:
+            continue
+        place = piece(pair.at[dz - 1], c)
+        place[...] = paired(dz, c).astype(BF16)
+        copy = remote(
+            place,
+            piece(from_z.at[dz - 1], c),
+            send.at[dz, 0, c],
+            recv.at[dz, 0, c],
+            grid.at(dz, 0),
+            grid.mp,
+        )
+        copy.start()
+        sent.append(copy)
     for c in range(CHUNKS):
         total = paired(0, c)
         for dz in range(1, grid.outer):
@@ -372,13 +446,14 @@
     ]
 
 
-def sum_gather_kernel(size, src, own, gathered, from_x, pair, from_z, s1, r1, mine, local, s2, r2):
+def sum_gather_kernel(size, src, own, gathered, from_x, pair, from_z, s1, r1, mine, local, *sems):
     grid = Grid(size)
     greet(grid.peers())
     sent = reduce_rows(grid, src, own, from_x, pair, from_z, s1, r1)
     mine[...] = own[...].astype(BF16)
-    started = gather_start(grid, mine, gathered, local.at[0], s2, r2)
-    gather_finish(grid, mine, gathered, started, s2, r2)
+    gather = Gather(grid, mine, gathered, local.at[0], *sems)
+    gather.start()
+    gather.finish()
     for copy in sent:
         copy.wait_send()
 
@@ -386,8 +461,6 @@
 def sum_gather(size, src):
     total, cols = src.shape
     rows = total // size
-    inner = inner_of(size)
-    sems = pltpu.SemaphoreType.DMA((size // inner, inner, CHUNKS))
     vmem = pl.BlockSpec(memory_space=pltpu.VMEM)
     return pl.pallas_call(
         functools.partial(sum_gather_kernel, size),
@@ -398,7 +471,8 @@
         in_specs=[vmem],
         out_specs=(vmem, pl.BlockSpec(memory_space=pl.ANY)),
         scratch_shapes=reduce_scratch(size, rows, cols)
-        + [pltpu.VMEM((rows, cols), BF16), pltpu.SemaphoreType.DMA((1,)), sems, sems],
+        + [pltpu.VMEM((rows, cols), BF16), pltpu.SemaphoreType.DMA((1,))]
+        + gather_scratch(size),
         compiler_params=pltpu.CompilerParams(
             collective_id=2, has_side_effects=True, vmem_limit_bytes=VMEM_LIMIT
         ),

time: 298 us -> 270 us (0.906)
  Pallas kernels: 242 us -> 215 us
    pallas_call x1, Pallas kernels: 104 us -> 92.2 us  [sum_gather(): pl.pallas_call(functools.partial(sum_gather_kernel, size), out_shape=(jax...]
    pallas_call x1, Pallas kernels: 62.8 us -> 52.7 us  [sum_only(): pl.pallas_call(functools.partial(sum_kernel, size), out_shape=(jax.ShapeD...]
    pallas_call x1, Pallas kernels: 54.3 us -> 47.9 us  [first(): pl.pallas_call(functools.partial(first_kernel, size), out_shape=(jax.Shap...]
where the time goes in v2:
time: 270 us
  Pallas kernels  215 us (80%)
  matrix products  30.7 us (11%)
  local copies, waits for them, and re-layouts  9.67 us (4%)
  between operations  9.25 us (3%)
  other arithmetic  5.37 us (2%)
    pallas_call x1, Pallas kernels, sum_gather(): pl.pallas_call(functools.partial(sum_gather_kernel, size), out_shape=(jax...  92.2 us
    pallas_call x1, Pallas kernels, sum_only(): pl.pallas_call(functools.partial(sum_kernel, size), out_shape=(jax.ShapeD...  52.7 us
    pallas_call x1, Pallas kernels, first(): pl.pallas_call(functools.partial(first_kernel, size), out_shape=(jax.Shap...  47.9 us
    pallas_call x2, Pallas kernels, curve(): pl.pallas_call(functools.partial(curve_kernel, ways, early), out_shape=tu...  22 us
    dot_general x2, matrix products, product(): lax.dot_general(attn, gdot, (((0,), (0,)), ((), ())), preferred_element_t...  14 us
    unnamed x32, local copies, waits for them, and re-layouts  8.48 us
    dot_general x1, matrix products, local(): hdot = jnp.dot(attn, once_all, preferred_element_type=F32)  6.31 us

profile of v2, /device:TPU:0, one launch (start us, length us, event | category | flops | bytes accessed | tf_op | source)
XLA Modules:
  0.0 269.8 jit_solution(11542499952618556558)
XLA Ops:
  0.0 2.4 multiply_reduce_fusion.4
  2.4 1.2 copy-done.3
  3.6 1.0 copy-done.4
  4.7 0.7 copy-done.5
  5.3 47.9 %attend_and_gather.1 = (bf16[512,2048]{1,0:T(8,128)(2,1)S(1)}, bf16[2048,896]{1,0:T(8,128)(2,1)}) custom-call(s32[1,4]{1,0:T(1,128)S(1)} %copy-done.5, bf16[128,2048]{1,0:T(8,128)(2,1)S(1)} %bitcast.27, bf16[512,1024]{1,0:T(8,128)(2,1)S(1)} %bitcast.25, bf16[512,1024]{1,0:T(8,128)(2,1)S(1)} %bitcast.26, bf16[256,896]{1,0:T(8,128)(2,1)S(1)} %get-tuple-element.34.src), custom_call_target="tpu_custom_call" | custom-call | tf_op jit(solution)/shard_map/attend_and_gather/pallas_call | solution.py:239
  53.3 5.2 %fusion.25 = f32[512,896]{1,0:T(8,128)S(1)} fusion(bf16[512,2048]{1,0:T(8,128)(2,1)S(1)} %get-tuple-element.16, bf16[2048,896]{1,0:T(8,128)(2,1)} %get-tuple-element.17), kind=kOutput, calls=%fused_computation.55 | convolution fusion | flops 1879048192 | bytes 7602176 | tf_op jit(solution)/shard_map/dot_general | solution.py:558
  58.5 2.5 multiply_reduce_fusion.2
  61.3 0.4 convolution_convert_fusion.4
  61.7 1.5 copy-done.11
  64.1 12.1 %curve_early.1 = (bf16[512,256]{1,0:T(8,128)(2,1)S(1)}, f32[128,128]{1,0:T(8,128)S(1)}, f32[128,128]{1,0:T(8,128)S(1)}, f32[8,128]{1,0:T(8,128)}) custom-call(bf16[512,384]{1,0:T(8,128)(2,1)S(1)} %fusion.11.refs_0_, s32[512,1]{1,0:T(8,128)S(1)} %copy.28.refs_1_), custom_call_target="tpu_custom_call" | custom-call | tf_op jit(solution)/shard_map/curve_early/pallas_call | solution.py:352
  76.2 0.4 fusion.16
  76.6 6.7 %convolution_convert_fusion.1.src = bf16[2048,896]{1,0:T(8,128)(2,1)} fusion(bf16[512,2048]{1,0:T(8,128)(2,1)} %copy-done.7, f32[512,896]{1,0:T(8,128)} %copy-done.10, f32[512,896]{1,0:T(8,128)S(1)} %get-tuple-element.45, bf16[896,128]{1,0:T(8,128)(2,1)S(1)} %copy-done, f32[512]{0:T(512)S(1)} %get-tuple-element.32, f32[512]{0:T(512)S(1)} %get-tuple-element.31, ...), kind=kOutput, calls=%fused_computation.1 | convolution fusion | flops 2001076224 | bytes 9805824 | tf_op jit(solution)/shard_map/dot_general | solution.py:556
  83.3 92.2 %sum_and_gather.1 = (f32[256,896]{1,0:T(8,128)S(1)}, bf16[2048,896]{1,0:T(8,128)(2,1)S(1)}) custom-call(bf16[2048,896]{1,0:T(8,128)(2,1)} %convolution_convert_fusion.1.src), custom_call_target="tpu_custom_call" | custom-call | tf_op jit(solution)/shard_map/sum_and_gather/pallas_call | solution.py:465
  175.5 1.8 copy-done.6
  177.3 0.8 multiply_reduce_fusion.3
  180.7 6.3 %multiply_reduce_fusion = (f32[512]{0:T(512)S(1)}, f32[512,896]{1,0:T(8,128)}) fusion(f32[512,896]{1,0:T(8,128)S(1)} %get-tuple-element.45, bf16[512,2048]{1,0:T(8,128)(2,1)} %copy-done.7, bf16[2048,896]{1,0:T(8,128)(2,1)} %copy-done.6), kind=kOutput, calls=%fused_computation.4 | convolution fusion | flops 1879965184 | bytes 9439232 | tf_op jit(solution)/shard_map/dot_general | solution.py:564
  191.1 1.9 convolution_convert_fusion.2
  193.1 9.8 %curve_late.1 = (bf16[512,256]{1,0:T(8,128)(2,1)S(1)}, f32[8,128]{1,0:T(8,128)S(1)}) custom-call(bf16[512,256]{1,0:T(8,128)(2,1)S(1)} %fusion.12.refs_0_, s32[512,1]{1,0:T(8,128)S(1)} %copy.28.refs_1_, f32[128,128]{1,0:T(8,128)S(1)} %get-tuple-element.21.refs_2_, f32[128,128]{1,0:T(8,128)S(1)} %get-tuple-element.22.refs_3_), custom_call_target="tpu_custom_call" | custom-call | tf_op jit(solution)/shard_map/curve_late/pallas_call | solution.py:352
  202.9 0.4 fusion.14
  203.4 7.3 %convolution_convert_fusion.src = bf16[2048,896]{1,0:T(8,128)(2,1)} fusion(bf16[512,2048]{1,0:T(8,128)(2,1)} %copy-done.7, f32[512,896]{1,0:T(8,128)} %get-tuple-element.47, f32[512,896]{1,0:T(8,128)} %copy-done.9, bf16[896,128]{1,0:T(8,128)(2,1)S(1)} %copy-done, f32[512]{0:T(512)S(1)} %get-tuple-element.30, f32[512]{0:T(512)S(1)} %get-tuple-element.29, ...), kind=kOutput, calls=%fused_computation | convolution fusion | flops 2001076224 | bytes 9805824 | tf_op jit(solution)/shard_map/dot_general | solution.py:556
  210.7 2.0 copy-done.1
  212.7 52.7 %sum_rows.1 = (f32[256,896]{1,0:T(8,128)S(1)}, f32[8,128]{1,0:T(8,128)S(1)}) custom-call(bf16[2048,896]{1,0:T(8,128)(2,1)S(1)} %copy-done.1, f32[8,128]{1,0:T(8,128)S(1)} %get-tuple-element.24.scalars), custom_call_target="tpu_custom_call" | custom-call | tf_op jit(solution)/shard_map/sum_rows/pallas_call | solution.py:506
  265.4 0.6 fusion.24
  268.7 1.1 divide_add_fusion
  (42 shorter events, 1.4 us)
Async XLA Ops:
  0.0 61.3 %copy-start = (bf16[896,128]{1,0:T(8,128)(2,1)S(1)}, bf16[896,128]{1,0:T(8,128)(2,1)}, u32[]{:S(2)}) copy-start(bf16[896,128]{1,0:T(8,128)(2,1)} %param.16) | copy-start | bytes 688132
  0.0 2.4 copy-start.2
  2.4 1.2 copy-start.3
  3.6 1.0 copy-start.4
  4.7 0.7 copy-start.5
  53.3 5.2 %copy-start.7 = (bf16[512,2048]{1,0:T(8,128)(2,1)}, bf16[512,2048]{1,0:T(8,128)(2,1)S(1)}, u32[]{:S(2)}) copy-start(bf16[512,2048]{1,0:T(8,128)(2,1)S(1)} %get-tuple-element.16) | copy-start | bytes 6291460
  53.3 5.2 %copy-start.14 = (bf16[2048,896]{1,0:T(8,128)(2,1)S(1)}, bf16[2048,896]{1,0:T(8,128)(2,1)}, u32[]{:S(2)}) copy-start(bf16[2048,896]{1,0:T(8,128)(2,1)} %param.14) | copy-start | bytes 11010052
  53.3 5.2 %copy-start.15 = (bf16[1,512,896]{2,1,0:T(8,128)(2,1)S(1)}, bf16[1,512,896]{2,1,0:T(8,128)(2,1)}, u32[]{:S(2)}) copy-start(bf16[1,512,896]{2,1,0:T(8,128)(2,1)} %param.13) | copy-start | bytes 2752516
  58.5 2.6 copy-start.10
  58.5 2.8 %copy-start.12 = (f32[896]{0:T(1024)S(1)}, f32[896]{0:T(1024)}, u32[]{:S(2)}) copy-start(f32[896]{0:T(1024)} %param.15) | copy-start | bytes 10756
  61.1 119.6 %copy-start.9 = (f32[512,896]{1,0:T(8,128)}, f32[512,896]{1,0:T(8,128)S(1)}, u32[]{:S(2)}) copy-start(f32[512,896]{1,0:T(8,128)S(1)} %get-tuple-element.45) | copy-start | bytes 5505028
  61.3 1.9 copy-start.11
  63.2 0.7 copy-start.13
  175.5 1.8 copy-start.6
  210.7 2.0 copy-start.1
  212.7 56.0 %copy-start.8 = (f32[256,896]{1,0:T(8,128)S(1)}, f32[256,896]{1,0:T(8,128)}, u32[]{:S(2)}) copy-start(f32[256,896]{1,0:T(8,128)} %param.17) | copy-start | bytes 2752516

commit v3 on v2

--- a/solution.py
+++ b/solution.py
@@ -21,7 +21,8 @@
 MESH = pl.DeviceIdType.MESH
 VMEM_LIMIT = 48 * 1024 * 1024
 CHUNKS = 2
-AHEAD = 2
+STEPS = 4
+LANES = 128
 F32 = jnp.float32
 BF16 = jnp.bfloat16
 
@@ -126,8 +127,9 @@
                 self.aside(self.own(c), 1, 0, dx, c).start()
         me = self.grid.at(0, 0)
         whole = self.dst.at[pl.ds(pl.multiple_of(me * self.rows, self.rows), self.rows)]
-        self.kept = pltpu.make_async_copy(self.src, whole, self.local)
-        self.kept.start()
+        kept = pltpu.make_async_copy(self.src, whole, self.local)
+        kept.start()
+        kept.wait()
 
     def take(self, way, hops, c):
         piece = self.block(way, hops, 0, c)
@@ -153,22 +155,39 @@
             for dx in range(1, self.grid.inner):
                 self.aside(piece, way, hops, dx, c).wait_send()
 
+    def each(self, act, hops):
+        for c in range(CHUNKS):
+            for way in (1, -1):
+                pl.when(self.arrives(way, hops))(lambda way=way, c=c: act(way, hops, c))
+
+    def line_in(self, hops):
+        self.each(self.take, hops)
+
+    def side_in(self, hops):
+        if hops:
+            self.each(self.take_aside, hops)
+        else:
+            for c in range(CHUNKS):
+                self.take_aside(1, 0, c)
+
+    def use(self, hops, dx, apply):
+        x = lax.rem(self.grid.x + (dx + self.grid.inner), self.grid.inner)
+        for way in (1, -1) if hops else (1,):
+            z = self.grid.z - hops * way
+            pl.when(self.arrives(way, hops))(lambda z=z: apply(z * self.grid.inner + x))
+
+    def use_side(self, hops, apply):
+        for dx in range(1, self.grid.inner):
+            self.use(hops, -dx, apply)
+
     def finish(self):
-        outer = self.grid.outer
-        for act in (self.take, self.take_aside, self.settle):
-            for hops in range(outer):
-                if hops == 0 and act == self.take:
-                    continue
+        for hops in range(self.grid.outer):
+            if hops:
+                self.each(self.settle, hops)
+            else:
                 for c in range(CHUNKS):
                     for way in (1, -1):
-                        if hops == 0:
-                            if act == self.settle or way > 0:
-                                act(way, hops, c)
-                        else:
-                            pl.when(self.arrives(way, hops))(
-                                lambda act=act, way=way, hops=hops, c=c: act(way, hops, c)
-                            )
-        self.kept.wait()
+                        self.settle(way, 0, c)
 
 
 def gather_scratch(size):
@@ -179,7 +198,34 @@
     return [line, line, side, side]
 
 
-def first_kernel(size, starts, query, key, value, src, attn, gathered, mine, local, send_m, recv_m, *sems):
+def times_shards(attn, gathered, out, rows):
+    tokens = attn.shape[0]
+    tile = min(tokens, 128)
+    if rows % LANES:
+        return lambda device: None
+
+    def apply(device):
+        span = pl.ds(pl.multiple_of(device * rows, rows), rows)
+
+        def body(t, carry):
+            here = pl.ds(pl.multiple_of(t * tile, tile), tile)
+            out[here, :] += jnp.dot(attn[here, span], gathered[span, :], preferred_element_type=F32)
+            return carry
+
+        lax.fori_loop(0, tokens // tile, body, 0)
+
+    return apply
+
+
+def times_whole(attn, gathered, out, rows):
+    if rows % LANES:
+        out[...] = jnp.dot(attn[...], gathered[...], preferred_element_type=F32)
+
+
+def first_kernel(
+    size, starts, query_in, key_in, value_in, src, stream_in, proj_in, attn, h_out, hdot,
+    query, key, value, stream, proj, gathered, mine, loads, local, send_m, recv_m, *sems
+):
     grid = Grid(size)
     q_rows, width = query.shape
     num_k = key.shape[0]
@@ -187,9 +233,15 @@
     dp = lax.axis_index("dp")
     mp = grid.mp
     others = [lax.rem(mp + d, ways) for d in range(1, ways)]
+    pairs = ((query_in, query), (key_in, key), (value_in, value), (stream_in, stream), (proj_in, proj))
+    loading = [pltpu.make_async_copy(there, here, loads.at[i]) for i, (there, here) in enumerate(pairs)]
+    for copy in loading:
+        copy.start()
     greet(grid.peers() + [(dp, other) for other in others])
     gather = Gather(grid, src, gathered, local.at[0], *sems)
     gather.start()
+    for copy in loading[:3]:
+        copy.wait()
 
     q_pos = mp * q_rows + lax.broadcasted_iota(jnp.int32, (q_rows, num_k), 0)
     k_pos = lax.broadcasted_iota(jnp.int32, (q_rows, num_k), 1)
@@ -212,6 +264,8 @@
         weights = (expo / jnp.sum(expo, -1, keepdims=True)).astype(BF16)
         out = jnp.dot(weights, value[:, g * HD : (g + 1) * HD], preferred_element_type=F32)
         mine[:, h * HD : (h + 1) * HD] = out.astype(BF16)
+        if h == HQ - 3 and grid.outer > 1:
+            gather.line_in(1)
 
     def rows_of(device):
         return attn.at[pl.ds(pl.multiple_of(device * q_rows, q_rows), q_rows)]
@@ -223,29 +277,57 @@
         copy.start()
     own = pltpu.make_async_copy(mine, rows_of(mp), local.at[1])
     own.start()
-    gather.finish()
+    hdot[...] = jnp.zeros_like(hdot)
+    for hops in range(2, grid.outer):
+        gather.line_in(hops)
+    own.wait()
     for d, other in enumerate(others):
         place = rows_of(lax.rem(mp + (ways - 1 - d), ways))
         remote(place, place, send_m.at[d], recv_m.at[d], dp, other).wait_recv()
-    own.wait()
+    for copy in loading[3:]:
+        copy.wait()
+    tile = min(num_k, 128)
+
+    def body(t, carry):
+        here = pl.ds(pl.multiple_of(t * tile, tile), tile)
+        h_out[here, :] = stream[here, :].astype(F32) + jnp.dot(
+            attn[here, :], proj[...], preferred_element_type=F32
+        )
+        return carry
+
+    lax.fori_loop(0, num_k // tile, body, 0)
+    apply = times_shards(attn, gathered, hdot, src.shape[0])
+    for hops in range(grid.outer):
+        gather.use(hops, 0, apply)
+    for hops in range(grid.outer):
+        gather.side_in(hops)
+        gather.use_side(hops, apply)
+    times_whole(attn, gathered, hdot, src.shape[0])
+    gather.finish()
     for copy in sent:
         copy.wait_send()
 
 
-def first(size, ways, starts, query, key, value, src):
+def first(size, ways, starts, query, key, value, src, stream, proj):
     rows, cols = src.shape
+    tokens = key.shape[0]
     vmem = pl.BlockSpec(memory_space=pltpu.VMEM)
     place = pl.BlockSpec(memory_space=pl.ANY)
+    loaded = (query, key, value, stream, proj)
     return pl.pallas_call(
         functools.partial(first_kernel, size),
         out_shape=(
-            jax.ShapeDtypeStruct((key.shape[0], query.shape[1]), BF16),
-            jax.ShapeDtypeStruct((rows * size, cols), BF16),
+            jax.ShapeDtypeStruct((tokens, query.shape[1]), BF16),
+            jax.ShapeDtypeStruct((tokens, cols), F32),
+            jax.ShapeDtypeStruct((tokens, cols), F32),
         ),
-        in_specs=[pl.BlockSpec(memory_space=pltpu.SMEM), vmem, vmem, vmem, place],
-        out_specs=(place, place),
-        scratch_shapes=[
+        in_specs=[pl.BlockSpec(memory_space=pltpu.SMEM), place, place, place, vmem, place, place],
+        out_specs=(vmem, vmem, vmem),
+        scratch_shapes=[pltpu.VMEM(array.shape, BF16) for array in loaded]
+        + [
+            pltpu.VMEM((rows * size, cols), BF16),
             pltpu.VMEM(query.shape, BF16),
+            pltpu.SemaphoreType.DMA((len(loaded),)),
             pltpu.SemaphoreType.DMA((2,)),
             pltpu.SemaphoreType.DMA((ways,)),
             pltpu.SemaphoreType.DMA((ways,)),
@@ -255,7 +337,7 @@
             collective_id=0, has_side_effects=True, vmem_limit_bytes=VMEM_LIMIT
         ),
         name="attend_and_gather",
-    )(starts, query, key, value, src)
+    )(starts, query, key, value, src, stream, proj)
 
 
 def curve_kernel(ways, early, *refs):
@@ -322,8 +404,10 @@
     columns = jnp.where(lane == 1, coeff - coeff_high, columns)
     columns = jnp.where(lane == 2, pull_high, columns)
     columns = jnp.where(lane == 3, pull - pull_high, columns)
-    mine[:, :TAGS] = mixed.astype(BF16)
-    mine[:, TAGS:] = columns.astype(BF16)
+    mixed_high = mixed.astype(BF16)
+    mine[:, :TAGS] = mixed_high
+    mine[:, TAGS : 2 * TAGS] = (mixed - mixed_high.astype(F32)).astype(BF16)
+    mine[:, 2 * TAGS :] = columns.astype(BF16)
     back = [
         remote(mine, packed.at[rows_of(mp)], s2.at[d], r2.at[d], dp, other)
         for d, other in enumerate(others)
@@ -344,7 +428,7 @@
     rows = tokens // ways
     vmem = pl.BlockSpec(memory_space=pltpu.VMEM)
     operands = (part, tags) if early else (part, tags) + state
-    out_shape = [jax.ShapeDtypeStruct((tokens, 2 * TAGS), BF16)]
+    out_shape = [jax.ShapeDtypeStruct((tokens, 3 * TAGS), BF16)]
     if early:
         out_shape += [jax.ShapeDtypeStruct((rows, TAGS), F32)] * 2
     out_shape += [jax.ShapeDtypeStruct((8, TAGS), F32)]
@@ -356,7 +440,7 @@
         out_specs=(vmem,) * len(out_shape),
         scratch_shapes=[
             pltpu.VMEM((ways - 1, rows, width), BF16),
-            pltpu.VMEM((rows, 2 * TAGS), BF16),
+            pltpu.VMEM((rows, 3 * TAGS), BF16),
             sems,
             sems,
             sems,
@@ -369,118 +453,193 @@
     )(*operands)
 
 
-def reduce_rows(grid, src, own, from_x, pair, from_z, send, recv):
-    rows = own.shape[0]
-    step = rows // CHUNKS
+def reduce_rows(grid, attn, gdot, own, full, away, kept, from_x, out, from_z, s_x, r_x, s_z, r_z):
+    rows, cols = own.shape
+    step = rows // STEPS
+    outer, inner = grid.outer, grid.inner
     sent = []
+    plans = []
+    for z in range(outer):
+        plan = [(k, way) for k in range(outer - 1, 0, -1) for way in (1, -1) if 0 <= z + k * way < outer]
+        plans.append(plan + [(0, 1)])
+
+    def pick(values):
+        out = jnp.int32(values[0])
+        for z in range(1, outer):
+            out = jnp.where(grid.z == z, jnp.int32(values[z]), out)
+        return out
+
+    dists = [pick([plan[j][0] for plan in plans]) for j in range(outer)]
+    ways = [pick([plan[j][1] for plan in plans]) for j in range(outer)]
 
     def piece(ref, c):
         return ref.at[pl.ds(c * step, step)]
 
-    order = [(dz, c) for dz in list(range(1, grid.outer)) + [0] for c in range(CHUNKS)]
-    queue = list(order)
-
-    def feed():
-        if queue:
-            dz, c = queue.pop(0)
-            for dx in range(1, grid.inner):
+    def columns_times(span):
+        return lax.dot_general(
+            attn[:, span], gdot[...], (((0,), (0,)), ((), ())), preferred_element_type=F32
+        )
+
+    if rows % LANES:
+        for start in range(0, full.shape[0], LANES):
+            full[start : start + LANES, :] = columns_times(pl.ds(start, LANES))
+
+    def product(j, dx):
+        z = grid.z + dists[j] * ways[j]
+        device = z * inner + lax.rem(grid.x + dx, inner)
+        span = pl.ds(pl.multiple_of(device * rows, rows), rows)
+        return full[span, :] if rows % LANES else columns_times(span)
+
+    def produce(j):
+        for dx in range(1, inner):
+            away[j, dx - 1] = product(j, dx).astype(BF16)
+
+    def keep(j):
+        kept[j] = product(j, 0)
+
+    def over(j, dx, c):
+        return remote(
+            piece(away.at[j, dx - 1], c),
+            piece(from_x.at[j, dx - 1], c),
+            s_x.at[j, dx, c],
+            r_x.at[j, dx, c],
+            grid.at(0, dx),
+            grid.mp,
+        )
+
+    def feed(j, c):
+        for dx in range(1, inner):
+            copy = over(j, dx, c)
+            copy.start()
+            sent.append(copy)
+
+    produce(0)
+    for c in range(STEPS):
+        feed(0, c)
+    keep(0)
+    for j in range(outer):
+        last = j == outer - 1
+        if not last:
+            produce(j + 1)
+        k, way = dists[j], ways[j]
+        lane = (way + 1) // 2
+        behind = grid.z - way
+        follows = (behind >= 0) & (behind < outer)
+        ahead = (grid.z + way) * inner + grid.x
+        for c in range(STEPS):
+            total = piece(kept.at[j], c)[...]
+            for dx in range(1, inner):
+                over(j, dx, c).wait_recv()
+                total = total + piece(from_x.at[j, dx - 1], c)[...].astype(F32)
+            if not last:
+                feed(j + 1, c)
+            if not last:
+                place = piece(out.at[j], c)
+                came = piece(from_z.at[lane, k], c)
+
+                @pl.when(follows)
+                def _():
+                    remote(came, came, s_z.at[j, c], r_z.at[lane, k, c], ahead, grid.mp).wait_recv()
+                    place[...] = (total + came[...].astype(F32)).astype(BF16)
+
+                @pl.when(jnp.logical_not(follows))
+                def _():
+                    place[...] = total.astype(BF16)
+
                 copy = remote(
-                    part_rows(src, grid.at(dz, dx), rows, c),
-                    piece(from_x.at[dz, dx - 1], c),
-                    send.at[dz, dx, c],
-                    recv.at[dz, dx, c],
-                    grid.at(0, dx),
-                    grid.mp,
+                    place, piece(from_z.at[lane, k - 1], c), s_z.at[j, c], r_z.at[lane, k - 1, c], ahead, grid.mp
                 )
                 copy.start()
                 sent.append(copy)
-
-    for _ in range(AHEAD):
-        feed()
-
-    def paired(dz, c):
-        total = part_rows(src, grid.at(dz, 0), rows, c)[...].astype(F32)
-        for dx in range(1, grid.inner):
-            place = piece(from_x.at[dz, dx - 1], c)
-            remote(place, place, send.at[dz, dx, c], recv.at[dz, dx, c], grid.at(0, dx), grid.mp).wait_recv()
-            if dx == grid.inner - 1:
-                feed()
-            total = total + place[...].astype(F32)
-        return total
-
-    for dz, c in order:
-        if dz == 0:
-            continue
-        place = piece(pair.at[dz - 1], c)
-        place[...] = paired(dz, c).astype(BF16)
-        copy = remote(
-            place,
-            piece(from_z.at[dz - 1], c),
-            send.at[dz, 0, c],
-            recv.at[dz, 0, c],
-            grid.at(dz, 0),
-            grid.mp,
-        )
-        copy.start()
-        sent.append(copy)
-    for c in range(CHUNKS):
-        total = paired(0, c)
-        for dz in range(1, grid.outer):
-            place = piece(from_z.at[dz - 1], c)
-            remote(place, place, send.at[dz, 0, c], recv.at[dz, 0, c], grid.at(dz, 0), grid.mp).wait_recv()
-            total = total + place[...].astype(F32)
-        piece(own, c)[...] = total
+            else:
+                piece(own, c)[...] = total
+        if not last:
+            keep(j + 1)
+    for c in range(STEPS):
+        for lane in range(2):
+            side = grid.z + (1 - 2 * lane)
+            came = piece(from_z.at[lane, 0], c)
+
+            @pl.when((side >= 0) & (side < outer))
+            def _():
+                remote(
+                    came, came, s_z.at[0, c], r_z.at[lane, 0, c], side * inner + grid.x, grid.mp
+                ).wait_recv()
+                piece(own, c)[...] += came[...].astype(F32)
     return sent
 
 
 def reduce_scratch(size, rows, cols):
     inner = inner_of(size)
     outer = size // inner
-    sems = pltpu.SemaphoreType.DMA((outer, inner, CHUNKS))
     return [
+        pltpu.VMEM((size * rows, cols) if rows % LANES else (8, LANES), F32),
+        pltpu.VMEM((outer, inner - 1, rows, cols), BF16),
+        pltpu.VMEM((outer, rows, cols), F32),
         pltpu.VMEM((outer, inner - 1, rows, cols), BF16),
         pltpu.VMEM((outer - 1, rows, cols), BF16),
-        pltpu.VMEM((outer - 1, rows, cols), BF16),
-        sems,
-        sems,
+        pltpu.VMEM((2, outer, rows, cols), BF16),
+        pltpu.SemaphoreType.DMA((outer, inner, STEPS)),
+        pltpu.SemaphoreType.DMA((outer, inner, STEPS)),
+        pltpu.SemaphoreType.DMA((outer, STEPS)),
+        pltpu.SemaphoreType.DMA((2, outer, STEPS)),
     ]
 
 
-def sum_gather_kernel(size, src, own, gathered, from_x, pair, from_z, s1, r1, mine, local, *sems):
+REDUCE_REFS = 10
+
+
+def sum_gather_kernel(size, attn, gdot, own, hdot, gathered, mine, local, *refs):
     grid = Grid(size)
     greet(grid.peers())
-    sent = reduce_rows(grid, src, own, from_x, pair, from_z, s1, r1)
+    sent = reduce_rows(grid, attn, gdot, own, *refs[:REDUCE_REFS])
     mine[...] = own[...].astype(BF16)
-    gather = Gather(grid, mine, gathered, local.at[0], *sems)
+    gather = Gather(grid, mine, gathered, local.at[0], *refs[REDUCE_REFS:])
     gather.start()
+    hdot[...] = jnp.zeros_like(hdot)
+    apply = times_shards(attn, gathered, hdot, own.shape[0])
+    gather.use(0, 0, apply)
+    for hops in range(1, grid.outer):
+        gather.line_in(hops)
+        gather.use(hops, 0, apply)
+        gather.side_in(hops - 1)
+        gather.use_side(hops - 1, apply)
+    gather.side_in(grid.outer - 1)
+    gather.use_side(grid.outer - 1, apply)
+    times_whole(attn, gathered, hdot, own.shape[0])
     gather.finish()
     for copy in sent:
         copy.wait_send()
 
 
-def sum_gather(size, src):
-    total, cols = src.shape
+def sum_gather(size, attn, gdot):
+    tokens, total = attn.shape
+    cols = gdot.shape[1]
     rows = total // size
     vmem = pl.BlockSpec(memory_space=pltpu.VMEM)
     return pl.pallas_call(
         functools.partial(sum_gather_kernel, size),
         out_shape=(
             jax.ShapeDtypeStruct((rows, cols), F32),
-            jax.ShapeDtypeStruct((total, cols), BF16),
+            jax.ShapeDtypeStruct((tokens, cols), F32),
         ),
-        in_specs=[vmem],
-        out_specs=(vmem, pl.BlockSpec(memory_space=pl.ANY)),
-        scratch_shapes=reduce_scratch(size, rows, cols)
-        + [pltpu.VMEM((rows, cols), BF16), pltpu.SemaphoreType.DMA((1,))]
+        in_specs=[vmem, vmem],
+        out_specs=(vmem, vmem),
+        scratch_shapes=[
+            pltpu.VMEM((total, cols), BF16),
+            pltpu.VMEM((rows, cols), BF16),
+            pltpu.SemaphoreType.DMA((1,)),
+        ]
+        + reduce_scratch(size, rows, cols)
         + gather_scratch(size),
         compiler_params=pltpu.CompilerParams(
             collective_id=2, has_side_effects=True, vmem_limit_bytes=VMEM_LIMIT
         ),
         name="sum_and_gather",
-    )(src)
-
-
-def sum_kernel(size, src, scalars, own, scalar_sum, from_x, pair, from_z, s1, r1, got, s2, r2):
+    )(attn, gdot)
+
+
+def sum_kernel(size, attn, gdot, scalars, own, scalar_sum, got, s2, r2, *refs):
     grid = Grid(size)
     others = [lax.rem(lax.axis_index("dp") + d, size) for d in range(1, size)]
     greet([(other, grid.mp) for other in others])
@@ -489,7 +648,7 @@
     ]
     for copy in small:
         copy.start()
-    sent = reduce_rows(grid, src, own, from_x, pair, from_z, s1, r1)
+    sent = reduce_rows(grid, attn, gdot, own, *refs)
     total = scalars[...]
     for d, copy in enumerate(small):
         copy.wait_recv()
@@ -499,9 +658,9 @@
         copy.wait_send()
 
 
-def sum_only(size, src, scalars):
-    total, cols = src.shape
-    rows = total // size
+def sum_only(size, attn, gdot, scalars):
+    cols = gdot.shape[1]
+    rows = attn.shape[1] // size
     vmem = pl.BlockSpec(memory_space=pltpu.VMEM)
     return pl.pallas_call(
         functools.partial(sum_kernel, size),
@@ -509,19 +668,19 @@
             jax.ShapeDtypeStruct((rows, cols), F32),
             jax.ShapeDtypeStruct(scalars.shape, F32),
         ),
-        in_specs=[vmem, vmem],
+        in_specs=[vmem, vmem, vmem],
         out_specs=(vmem, vmem),
-        scratch_shapes=reduce_scratch(size, rows, cols)
-        + [
+        scratch_shapes=[
             pltpu.VMEM((size - 1,) + scalars.shape, F32),
             pltpu.SemaphoreType.DMA((size - 1,)),
             pltpu.SemaphoreType.DMA((size - 1,)),
-        ],
+        ]
+        + reduce_scratch(size, rows, cols),
         compiler_params=pltpu.CompilerParams(
             collective_id=4, has_side_effects=True, vmem_limit_bytes=VMEM_LIMIT
         ),
         name="sum_rows",
-    )(src, scalars)
+    )(attn, gdot, scalars)
 
 
 def split_columns(values, tokens):
@@ -538,36 +697,40 @@
     count = HQ * HD * D
     tokens = keys.shape[1]
     tag_column = tags[0][:, None]
-    attn, rounded = first(
-        size, ways, starts, queries[0], keys[0], values[0], direction.astype(BF16)
+    attn, h_loc, hdot = first(
+        size, ways, starts, queries[0], keys[0], values[0], direction.astype(BF16), stream[0], out_proj
     )
-    h_loc = stream[0].astype(F32) + jnp.dot(attn, out_proj, preferred_element_type=F32)
+    tag_twice = jnp.concatenate([tag_proj, tag_proj], 1)
 
     def scores(value):
-        return jnp.dot((value * norm_gain).astype(BF16), tag_proj, preferred_element_type=F32).astype(BF16)
-
-    def product(packed, hdot):
-        mixed = packed[:, :TAGS]
-        columns = packed[:, TAGS : TAGS + 4].astype(F32)
+        value = value * norm_gain
+        high = lax.reduce_precision(value, 8, 7)
+        low = (value - high).astype(BF16)
+        return (
+            jnp.dot(high.astype(BF16), tag_proj, preferred_element_type=F32)
+            + jnp.dot(low, tag_proj, preferred_element_type=F32)
+        ).astype(BF16)
+
+    def tangent(packed, hdot):
+        columns = packed[:, 2 * TAGS : 2 * TAGS + 4].astype(F32)
         coeff = columns[:, 0:1] + columns[:, 1:2]
         pull = columns[:, 2:3] + columns[:, 3:4]
-        back = lax.dot_general(mixed, tag_proj, (((1,), (1,)), ((), ())), preferred_element_type=F32)
-        gdot = (back * norm_gain - coeff * h_loc - pull * hdot).astype(BF16)
-        return lax.dot_general(attn, gdot, (((0,), (0,)), ((), ())), preferred_element_type=F32).astype(BF16)
-
-    hdot = jnp.dot(attn, rounded, preferred_element_type=F32)
+        back = lax.dot_general(
+            packed[:, : 2 * TAGS], tag_twice, (((1,), (1,)), ((), ())), preferred_element_type=F32
+        )
+        return (back * norm_gain - coeff * h_loc - pull * hdot).astype(BF16)
+
     extra = split_columns([jnp.sum(h_loc * hdot, -1), jnp.sum(h_loc * h_loc, -1)], tokens)
     part = jnp.concatenate([scores(h_loc), scores(hdot), extra], 1)
     packed, zval, rscale, _ = curve(ways, part, tag_column, None, 1)
-    once, once_all = sum_gather(size, product(packed, hdot))
-
-    hdot = jnp.dot(attn, once_all, preferred_element_type=F32)
+    once, hdot = sum_gather(size, attn, tangent(packed, hdot))
+
     extra = split_columns(
         [jnp.sum(h_loc * hdot, -1), jnp.sum(direction * direction), jnp.sum(once * once)], tokens
     )
     part = jnp.concatenate([scores(hdot), extra], 1)
     packed, scalars = curve(ways, part, tag_column, (zval, rscale), 3)
-    twice, sums = sum_only(size, product(packed, hdot), scalars)
+    twice, sums = sum_only(size, attn, tangent(packed, hdot), scalars)
 
     early_norm = sums[0, 2] + sums[0, 3]
     product_sq = sums[0, 4] + sums[0, 5]

time: 270 us -> 249 us (0.922)
  matrix products: 30.7 us -> 6.85 us
  other arithmetic: 5.37 us -> 9.17 us
  Pallas kernels: 215 us -> 212 us
    dot_general x8, matrix products: 30.7 us -> 6.85 us  [the longest x3 4.49 us: scores(): jnp.dot(high.astype(BF16), tag_proj, preferred_element_type=F32)]
    pallas_call x1, Pallas kernels: 52.7 us -> 45.6 us  [sum_only(): pl.pallas_call(functools.partial(sum_kernel, size), out_shape=(jax.ShapeD...]
    pallas_call x2, Pallas kernels: 22 us -> 26.2 us  [curve(): pl.pallas_call(functools.partial(curve_kernel, ways, early), out_shape=tu...]
    reduce_sum x0 -> x2, other arithmetic: none -> 3.63 us  [local(): jnp.sum(h_loc * hdot, -1)]
    pallas_call x1, Pallas kernels: 47.9 us -> 51.1 us  [first(): pl.pallas_call(functools.partial(first_kernel, size), out_shape=(jax.Shap...]
    pallas_call x1, Pallas kernels: 92.2 us -> 89.3 us  [sum_gather(): pl.pallas_call(functools.partial(sum_gather_kernel, size), out_shape=(jax...]
    unnamed x32 -> x33, local copies, waits for them, and re-layouts: 8.48 us -> 7.91 us
where the time goes in v3:
time: 249 us; the launch traced here: 248 us
  Pallas kernels  212 us (85%)
  local copies, waits for them, and re-layouts  10.8 us (4%)
  between operations  9.18 us (4%)
  other arithmetic  9.17 us (4%)
  matrix products  6.85 us (3%)
    pallas_call x1, Pallas kernels, sum_gather(): pl.pallas_call(functools.partial(sum_gather_kernel, size), out_shape=(jax...  89.3 us
    pallas_call x1, Pallas kernels, first(): pl.pallas_call(functools.partial(first_kernel, size), out_shape=(jax.Shap...  51.1 us
    pallas_call x1, Pallas kernels, sum_only(): pl.pallas_call(functools.partial(sum_kernel, size), out_shape=(jax.ShapeD...  45.6 us
    pallas_call x2, Pallas kernels, curve(): pl.pallas_call(functools.partial(curve_kernel, ways, early), out_shape=tu...  26.2 us
    unnamed x33, local copies, waits for them, and re-layouts  7.91 us

profile of v3, /device:TPU:0, one launch (start us, length us, event | category | flops | bytes accessed | tf_op | source)
XLA Modules:
  0.0 248.3 jit_solution(1679171637827541856)
XLA Ops:
  0.0 0.9 copy.36.refs_1_
  0.9 1.0 constant_dynamic-update-slice_fusion.1
  1.9 1.0 constant_dynamic-update-slice_fusion
  2.9 2.5 %multiply_reduce_fusion.4 = (f32[]{:T(128)}, bf16[256,896]{1,0:T(8,128)(2,1)S(1)}) fusion(f32[256,896]{1,0:T(8,128)} %param.17), kind=kLoop, calls=%fused_computation.25 | loop fusion | flops 688127 | bytes 1376260 | tf_op jit(solution)/shard_map/reduce_sum | solution.py:729
  8.6 1.2 copy-done.4
  9.8 1.2 copy-done.5
  11.0 1.2 copy-done.6
  12.2 51.1 %attend_and_gather.1 = (bf16[512,2048]{1,0:T(8,128)(2,1)}, f32[512,896]{1,0:T(8,128)S(1)}, f32[512,896]{1,0:T(8,128)}) custom-call(s32[1,4]{1,0:T(1,128)S(1)} %copy-done.8, bf16[128,2048]{1,0:T(8,128)(2,1)S(1)} %bitcast.21, bf16[512,1024]{1,0:T(8,128)(2,1)S(1)} %bitcast.18, bf16[512,1024]{1,0:T(8,128)(2,1)S(1)} %bitcast.19, ...), custom_call_target="tpu_custom_call" | custom-call | tf_op jit(solution)/shard_map/attend_and_gather/pallas_call | solution.py:317
  63.3 1.9 multiply_reduce_fusion.2
  65.4 2.0 fusion.10
  68.8 15.4 %curve_early.1 = (bf16[512,384]{1,0:T(8,128)(2,1)S(1)}, f32[128,128]{1,0:T(8,128)S(1)}, f32[128,128]{1,0:T(8,128)S(1)}, f32[8,128]{1,0:T(8,128)}) custom-call(bf16[512,384]{1,0:T(8,128)(2,1)S(1)} %fusion.20.refs_0_, s32[512,1]{1,0:T(8,128)S(1)} %copy.36.refs_1_), custom_call_target="tpu_custom_call" | custom-call | tf_op jit(solution)/shard_map/curve_early/pallas_call | solution.py:436
  84.7 0.6 subtract_convert_fusion.1.gdot
  85.2 1.0 copy-done.2
  86.3 89.3 %sum_and_gather.1 = (f32[256,896]{1,0:T(8,128)S(1)}, f32[512,896]{1,0:T(8,128)S(1)}) custom-call(bf16[512,2048]{1,0:T(8,128)(2,1)S(1)} %copy-done.2, bf16[512,896]{1,0:T(8,128)(2,1)S(1)} %subtract_convert_fusion.1.gdot), custom_call_target="tpu_custom_call" | custom-call | tf_op jit(solution)/shard_map/sum_and_gather/pallas_call | solution.py:620
  175.6 1.2 copy-done
  176.8 0.9 multiply_reduce_fusion.3
  180.7 1.7 multiply_reduce_fusion
  182.7 2.0 fusion.11
  185.3 10.9 %curve_late.1 = (bf16[512,384]{1,0:T(8,128)(2,1)S(1)}, f32[8,128]{1,0:T(8,128)S(1)}) custom-call(bf16[512,256]{1,0:T(8,128)(2,1)S(1)} %fusion.21.refs_0_, s32[512,1]{1,0:T(8,128)S(1)} %copy.36.refs_1_, f32[128,128]{1,0:T(8,128)S(1)} %get-tuple-element.23.refs_2_, f32[128,128]{1,0:T(8,128)S(1)} %get-tuple-element.24.refs_3_), custom_call_target="tpu_custom_call" | custom-call | tf_op jit(solution)/shard_map/curve_late/pallas_call | solution.py:436
  196.6 0.6 subtract_convert_fusion.gdot
  197.2 1.0 copy-done.3
  198.2 45.6 %sum_rows.1 = (f32[256,896]{1,0:T(8,128)S(1)}, f32[8,128]{1,0:T(8,128)S(1)}) custom-call(bf16[512,2048]{1,0:T(8,128)(2,1)S(1)} %copy-done.3, bf16[512,896]{1,0:T(8,128)(2,1)S(1)} %subtract_convert_fusion.gdot, f32[8,128]{1,0:T(8,128)S(1)} %get-tuple-element.26.scalars), custom_call_target="tpu_custom_call" | custom-call | tf_op jit(solution)/shard_map/sum_rows/pallas_call | solution.py:665
  243.8 0.7 fusion.31
  247.1 1.1 divide_add_fusion
  (46 shorter events, 3.2 us)
Async XLA Ops:
  0.0 8.5 %copy-start.8 = (s32[1,4]{1,0:T(1,128)S(1)}, s32[1,4]{1,0:T(1,128)}, u32[]{:S(2)}) copy-start(s32[1,4]{1,0:T(1,128)} %starts.1) | copy-start | bytes 52
  0.0 8.5 %copy-start.7 = (bf16[1,128,2048]{2,1,0:T(8,128)(2,1)S(1)}, bf16[1,128,2048]{2,1,0:T(8,128)(2,1)}, u32[]{:S(2)}) copy-start(bf16[1,128,2048]{2,1,0:T(8,128)(2,1)} %param.10) | copy-start | bytes 1572868
  2.9 5.6 %copy-start.12 = (bf16[896,256]{1,0:T(8,128)(2,1)}, bf16[896,256]{1,0:T(8,128)(2,1)S(1)}, u32[]{:S(2)}) copy-start(bf16[896,256]{1,0:T(8,128)(2,1)S(1)} %constant_dynamic-update-slice_fusion) | copy-start | bytes 1376260
  8.5 1.2 copy-start.4
  9.8 1.2 copy-start.5
  11.0 1.2 copy-start.6
  63.3 2.1 copy-start.10
  63.3 2.1 copy-start.15
  65.4 2.1 copy-start.9
  68.8 15.9 %copy-start.13 = (bf16[896,256]{1,0:T(8,128)(2,1)S(1)}, bf16[896,256]{1,0:T(8,128)(2,1)}, u32[]{:S(2)}) copy-start(bf16[896,256]{1,0:T(8,128)(2,1)} %copy-done.12) | copy-start | bytes 1376260
  84.7 1.6 copy-start.2
  175.6 1.2 copy-start
  182.7 2.1 copy-start.1
  185.2 11.4 %copy-start.14 = (bf16[896,256]{1,0:T(8,128)(2,1)S(1)}, bf16[896,256]{1,0:T(8,128)(2,1)}, u32[]{:S(2)}) copy-start(bf16[896,256]{1,0:T(8,128)(2,1)} %copy-done.12) | copy-start | bytes 1376260
  196.6 1.6 copy-start.3
  198.2 48.9 %copy-start.11 = (f32[256,896]{1,0:T(8,128)S(1)}, f32[256,896]{1,0:T(8,128)}, u32[]{:S(2)}) copy-start(f32[256,896]{1,0:T(8,128)} %param.17) | copy-start | bytes 2752516

commit v4 on v3

--- a/solution.py
+++ b/solution.py
@@ -1,4 +1,5 @@
 import functools
+import types
 
 import jax
 import jax.numpy as jnp
@@ -19,7 +20,7 @@
 MEAN_EPS = 1e-06
 
 MESH = pl.DeviceIdType.MESH
-VMEM_LIMIT = 48 * 1024 * 1024
+VMEM_LIMIT = 58 * 1024 * 1024
 CHUNKS = 2
 STEPS = 4
 LANES = 128
@@ -222,27 +223,9 @@
         out[...] = jnp.dot(attn[...], gathered[...], preferred_element_type=F32)
 
 
-def first_kernel(
-    size, starts, query_in, key_in, value_in, src, stream_in, proj_in, attn, h_out, hdot,
-    query, key, value, stream, proj, gathered, mine, loads, local, send_m, recv_m, *sems
-):
-    grid = Grid(size)
-    q_rows, width = query.shape
-    num_k = key.shape[0]
-    ways = num_k // q_rows
-    dp = lax.axis_index("dp")
-    mp = grid.mp
-    others = [lax.rem(mp + d, ways) for d in range(1, ways)]
-    pairs = ((query_in, query), (key_in, key), (value_in, value), (stream_in, stream), (proj_in, proj))
-    loading = [pltpu.make_async_copy(there, here, loads.at[i]) for i, (there, here) in enumerate(pairs)]
-    for copy in loading:
-        copy.start()
-    greet(grid.peers() + [(dp, other) for other in others])
-    gather = Gather(grid, src, gathered, local.at[0], *sems)
-    gather.start()
-    for copy in loading[:3]:
-        copy.wait()
-
+def attend(ref, starts, mp, between):
+    q_rows = ref.query.shape[0]
+    num_k = ref.key.shape[0]
     q_pos = mp * q_rows + lax.broadcasted_iota(jnp.int32, (q_rows, num_k), 0)
     k_pos = lax.broadcasted_iota(jnp.int32, (q_rows, num_k), 1)
     q_file = jnp.zeros((q_rows, num_k), jnp.int32)
@@ -254,102 +237,55 @@
     for h in range(HQ):
         g = h // (HQ // HK)
         scores = lax.dot_general(
-            query[:, h * HD : (h + 1) * HD],
-            key[:, g * HD : (g + 1) * HD],
+            ref.query[:, h * HD : (h + 1) * HD],
+            ref.key[:, g * HD : (g + 1) * HD],
             (((1,), (1,)), ((), ())),
             preferred_element_type=F32,
         ) * (1.0 / HD**0.5)
         scores = 50.0 * jnp.tanh(scores / 50.0)
         expo = jnp.where(allowed, jnp.exp(scores), 0.0)
         weights = (expo / jnp.sum(expo, -1, keepdims=True)).astype(BF16)
-        out = jnp.dot(weights, value[:, g * HD : (g + 1) * HD], preferred_element_type=F32)
-        mine[:, h * HD : (h + 1) * HD] = out.astype(BF16)
-        if h == HQ - 3 and grid.outer > 1:
-            gather.line_in(1)
-
-    def rows_of(device):
-        return attn.at[pl.ds(pl.multiple_of(device * q_rows, q_rows), q_rows)]
-
-    sent = [
-        remote(mine, rows_of(mp), send_m.at[d], recv_m.at[d], dp, other) for d, other in enumerate(others)
-    ]
-    for copy in sent:
-        copy.start()
-    own = pltpu.make_async_copy(mine, rows_of(mp), local.at[1])
-    own.start()
-    hdot[...] = jnp.zeros_like(hdot)
-    for hops in range(2, grid.outer):
-        gather.line_in(hops)
-    own.wait()
-    for d, other in enumerate(others):
-        place = rows_of(lax.rem(mp + (ways - 1 - d), ways))
-        remote(place, place, send_m.at[d], recv_m.at[d], dp, other).wait_recv()
-    for copy in loading[3:]:
-        copy.wait()
-    tile = min(num_k, 128)
+        out = jnp.dot(weights, ref.value[:, g * HD : (g + 1) * HD], preferred_element_type=F32)
+        ref.mine[:, h * HD : (h + 1) * HD] = out.astype(BF16)
+        if h == HQ - 3:
+            between()
+
+
+def over_tokens(tokens, act):
+    tile = min(tokens, 128)
 
     def body(t, carry):
-        here = pl.ds(pl.multiple_of(t * tile, tile), tile)
-        h_out[here, :] = stream[here, :].astype(F32) + jnp.dot(
-            attn[here, :], proj[...], preferred_element_type=F32
-        )
+        act(pl.ds(pl.multiple_of(t * tile, tile), tile), tile)
         return carry
 
-    lax.fori_loop(0, num_k // tile, body, 0)
-    apply = times_shards(attn, gathered, hdot, src.shape[0])
-    for hops in range(grid.outer):
-        gather.use(hops, 0, apply)
-    for hops in range(grid.outer):
-        gather.side_in(hops)
-        gather.use_side(hops, apply)
-    times_whole(attn, gathered, hdot, src.shape[0])
-    gather.finish()
-    for copy in sent:
-        copy.wait_send()
-
-
-def first(size, ways, starts, query, key, value, src, stream, proj):
-    rows, cols = src.shape
-    tokens = key.shape[0]
-    vmem = pl.BlockSpec(memory_space=pltpu.VMEM)
-    place = pl.BlockSpec(memory_space=pl.ANY)
-    loaded = (query, key, value, stream, proj)
-    return pl.pallas_call(
-        functools.partial(first_kernel, size),
-        out_shape=(
-            jax.ShapeDtypeStruct((tokens, query.shape[1]), BF16),
-            jax.ShapeDtypeStruct((tokens, cols), F32),
-            jax.ShapeDtypeStruct((tokens, cols), F32),
-        ),
-        in_specs=[pl.BlockSpec(memory_space=pltpu.SMEM), place, place, place, vmem, place, place],
-        out_specs=(vmem, vmem, vmem),
-        scratch_shapes=[pltpu.VMEM(array.shape, BF16) for array in loaded]
-        + [
-            pltpu.VMEM((rows * size, cols), BF16),
-            pltpu.VMEM(query.shape, BF16),
-            pltpu.SemaphoreType.DMA((len(loaded),)),
-            pltpu.SemaphoreType.DMA((2,)),
-            pltpu.SemaphoreType.DMA((ways,)),
-            pltpu.SemaphoreType.DMA((ways,)),
-        ]
-        + gather_scratch(size),
-        compiler_params=pltpu.CompilerParams(
-            collective_id=0, has_side_effects=True, vmem_limit_bytes=VMEM_LIMIT
-        ),
-        name="attend_and_gather",
-    )(starts, query, key, value, src, stream, proj)
-
-
-def curve_kernel(ways, early, *refs):
-    if early:
-        part, tags, packed, z_out, r_out, extra_out, got, mine, s1, r1, s2, r2 = refs
-    else:
-        part, tags, z_in, r_in, packed, extra_out, got, mine, s1, r1, s2, r2 = refs
-    rows = part.shape[0] // ways
+    lax.fori_loop(0, tokens // tile, body, 0)
+
+
+def high_low(value):
+    high = value.astype(BF16).astype(F32)
+    return [high, value - high]
+
+
+def tag_scores(value, gain, tag):
+    high, low = high_low(value * gain)
+    out = jnp.dot(high.astype(BF16), tag, preferred_element_type=F32)
+    return (out + jnp.dot(low.astype(BF16), tag, preferred_element_type=F32)).astype(BF16)
+
+
+def columns_of(values, tile):
+    lane = lax.broadcasted_iota(jnp.int32, (tile, TAGS), 1)
+    out = jnp.zeros((tile, TAGS), F32)
+    for i, value in enumerate(values):
+        out = jnp.where(lane == i, value, out)
+    return out.astype(BF16)
+
+
+def exchange(ref, early, part, got, mine, packed, s1, r1, s2, r2):
     dp = lax.axis_index("dp")
     mp = lax.axis_index("mp")
+    rows = mine.shape[0]
+    ways = part.shape[0] // rows
     others = [lax.rem(mp + d, ways) for d in range(1, ways)]
-    greet([(dp, other) for other in others])
 
     def rows_of(device):
         return pl.ds(pl.multiple_of(device * rows, rows), rows)
@@ -364,28 +300,24 @@
     for d, copy in enumerate(sent):
         copy.wait_recv()
         total = total + got[d].astype(F32)
+    zdot = total[:, :TAGS]
+    extra = total[:, TAGS : 2 * TAGS]
     if early:
-        zval = total[:, :TAGS]
-        zdot = total[:, TAGS : 2 * TAGS]
-        extra = total[:, 2 * TAGS :]
+        zval = total[:, 2 * TAGS :]
         sumsq = extra[:, 2:3] + extra[:, 3:4]
         rscale = lax.rsqrt(sumsq / D + NORM_EPS)
-        z_out[...] = zval
-        r_out[...] = jnp.broadcast_to(rscale, r_out.shape)
+        ref.zval[...] = zval
+        ref.rscale[...] = jnp.broadcast_to(rscale, ref.rscale.shape)
     else:
-        zdot = total[:, :TAGS]
-        extra = total[:, TAGS:]
-        zval = z_in[...]
-        rscale = r_in[:, 0:1]
+        zval = ref.zval[...]
+        rscale = ref.rscale[:, 0:1]
+        ref.scalars[...] = extra[:8, :]
     along = extra[:, 0:1] + extra[:, 1:2]
-    extra_out[...] = extra[:8, :]
     tanh_val = jnp.tanh(rscale * zval / 30.0)
     slope = 1.0 - tanh_val * tanh_val
     expo = jnp.exp(30.0 * tanh_val)
     probs = expo / jnp.sum(expo, -1, keepdims=True)
-    lane = lax.broadcasted_iota(jnp.int32, zval.shape, 1)
-    onehot = (tags[rows_of(mp), :] == lane).astype(F32)
-    dlogit = probs - onehot
+    dlogit = probs - ref.onehot[rows_of(mp), :]
     wgrad = dlogit * slope
     rho = jnp.sum(wgrad * zval, -1, keepdims=True)
     cube = rscale * rscale * rscale / D
@@ -397,17 +329,10 @@
     rhodot = jnp.sum(wdot * zval + wgrad * zdot, -1, keepdims=True)
     mixed = rdot * wgrad + rscale * wdot
     coeff = rhodot * cube + 3.0 * rho * rscale * rscale * rdot / D
-    pull = rho * cube
-    coeff_high = coeff.astype(BF16).astype(F32)
-    pull_high = pull.astype(BF16).astype(F32)
-    columns = jnp.where(lane == 0, coeff_high, 0.0)
-    columns = jnp.where(lane == 1, coeff - coeff_high, columns)
-    columns = jnp.where(lane == 2, pull_high, columns)
-    columns = jnp.where(lane == 3, pull - pull_high, columns)
-    mixed_high = mixed.astype(BF16)
-    mine[:, :TAGS] = mixed_high
-    mine[:, TAGS : 2 * TAGS] = (mixed - mixed_high.astype(F32)).astype(BF16)
-    mine[:, 2 * TAGS :] = columns.astype(BF16)
+    high, low = high_low(mixed)
+    mine[:, :TAGS] = high.astype(BF16)
+    mine[:, TAGS : 2 * TAGS] = low.astype(BF16)
+    mine[:, 2 * TAGS :] = columns_of(high_low(coeff) + high_low(rho * cube), rows)
     back = [
         remote(mine, packed.at[rows_of(mp)], s2.at[d], r2.at[d], dp, other)
         for d, other in enumerate(others)
@@ -422,35 +347,249 @@
         copy.wait_send()
 
 
-def curve(ways, part, tags, state, collective_id):
-    early = state is None
-    tokens, width = part.shape
-    rows = tokens // ways
+def tangent(ref, packed, hdot):
+    def act(here, tile):
+        columns = packed[here, 2 * TAGS :].astype(F32)
+        coeff = columns[:, 0:1] + columns[:, 1:2]
+        pull = columns[:, 2:3] + columns[:, 3:4]
+        back = jnp.zeros((tile, ref.gain.shape[1]), F32)
+        for i in range(2):
+            back = back + lax.dot_general(
+                packed[here, i * TAGS : (i + 1) * TAGS],
+                ref.tag[...],
+                (((1,), (1,)), ((), ())),
+                preferred_element_type=F32,
+            )
+        gdot = back * ref.gain[...] - coeff * ref.h[here, :] - pull * hdot[here, :]
+        ref.gdot[here, :] = gdot.astype(BF16)
+
+    over_tokens(hdot.shape[0], act)
+
+
+def whole_kernel(size, names, *refs):
+    ref = types.SimpleNamespace(**dict(zip(names, refs)))
+    grid = Grid(size)
+    dp = lax.axis_index("dp")
+    mp = grid.mp
+    q_rows = ref.query.shape[0]
+    tokens = ref.key.shape[0]
+    ways = tokens // q_rows
+    rows = ref.direction.shape[0]
+    others = [lax.rem(mp + d, ways) for d in range(1, ways)]
+    far = [lax.rem(dp + d, size) for d in range(1, size)]
+    pairs = [
+        (ref.direction_in, ref.direction),
+        (ref.query_in, ref.query),
+        (ref.key_in, ref.key),
+        (ref.value_in, ref.value),
+        (ref.stream_in, ref.stream),
+        (ref.proj_in, ref.proj),
+    ]
+    loading = [pltpu.make_async_copy(there, here, ref.loads.at[i]) for i, (there, here) in enumerate(pairs)]
+    for copy in loading:
+        copy.start()
+    greet([(dp, other) for other in others] + [(other, mp) for other in far])
+    loading[0].wait()
+    ref.src[...] = ref.direction[...].astype(BF16)
+    gather = Gather(grid, ref.src, ref.gathered, ref.local.at[0], *[getattr(ref, n) for n in GATHER_A])
+    gather.start()
+    for copy in loading[1:4]:
+        copy.wait()
+
+    def between():
+        if grid.outer > 1:
+            gather.line_in(1)
+
+    attend(ref, ref.starts, mp, between)
+
+    def rows_of(device):
+        return ref.attn.at[pl.ds(pl.multiple_of(device * q_rows, q_rows), q_rows)]
+
+    sent = [
+        remote(ref.mine, rows_of(mp), ref.send_m.at[d], ref.recv_m.at[d], dp, other)
+        for d, other in enumerate(others)
+    ]
+    for copy in sent:
+        copy.start()
+    own = pltpu.make_async_copy(ref.mine, rows_of(mp), ref.local.at[1])
+    own.start()
+    tag_ids = lax.broadcasted_iota(jnp.int32, (TAGS, tokens), 0)
+    ref.onehot[...] = jnp.transpose((tag_ids == ref.tags[...]).astype(F32))
+    ref.hdot[...] = jnp.zeros_like(ref.hdot)
+    ref.hdot_late[...] = jnp.zeros_like(ref.hdot_late)
+    early_norm = jnp.sum(ref.direction[...] * ref.direction[...], keepdims=True)
+    for hops in range(2, grid.outer):
+        gather.line_in(hops)
+    own.wait()
+    for d, other in enumerate(others):
+        place = rows_of(lax.rem(mp + (ways - 1 - d), ways))
+        remote(place, place, ref.send_m.at[d], ref.recv_m.at[d], dp, other).wait_recv()
+    for copy in loading[4:]:
+        copy.wait()
+
+    def project(here, tile):
+        h = ref.stream[here, :].astype(F32) + jnp.dot(
+            ref.attn[here, :], ref.proj[...], preferred_element_type=F32
+        )
+        ref.h[here, :] = h
+        ref.part[here, 2 * TAGS :] = tag_scores(h, ref.gain[...], ref.tag[...])
+
+    over_tokens(tokens, project)
+    apply = times_shards(ref.attn, ref.gathered, ref.hdot, rows)
+    for hops in range(grid.outer):
+        gather.use(hops, 0, apply)
+    for hops in range(grid.outer):
+        gather.side_in(hops)
+        gather.use_side(hops, apply)
+    times_whole(ref.attn, ref.gathered, ref.hdot, rows)
+
+    def scores_early(here, tile):
+        h = ref.h[here, :]
+        hdot = ref.hdot[here, :]
+        ref.part[here, :TAGS] = tag_scores(hdot, ref.gain[...], ref.tag[...])
+        ref.part[here, TAGS : 2 * TAGS] = columns_of(
+            high_low(jnp.sum(h * hdot, -1, keepdims=True)) + high_low(jnp.sum(h * h, -1, keepdims=True)), tile
+        )
+
+    over_tokens(tokens, scores_early)
+    exchange(ref, True, ref.part, ref.got, ref.mixed, ref.packed, *[getattr(ref, n) for n in SWAP_A])
+    gather.finish()
+    for copy in sent:
+        copy.wait_send()
+    tangent(ref, ref.packed, ref.hdot)
+    sent = reduce_rows(grid, ref.attn, ref.gdot, ref.once, *[getattr(ref, n) for n in REDUCE_A])
+    ref.src_late[...] = ref.once[...].astype(BF16)
+    gather = Gather(
+        grid, ref.src_late, ref.gathered_late, ref.local.at[0], *[getattr(ref, n) for n in GATHER_B]
+    )
+    gather.start()
+    product_sq = jnp.sum(ref.once[...] * ref.once[...], keepdims=True)
+    apply = times_shards(ref.attn, ref.gathered_late, ref.hdot_late, rows)
+    gather.use(0, 0, apply)
+    for hops in range(1, grid.outer):
+        gather.line_in(hops)
+        gather.use(hops, 0, apply)
+        gather.side_in(hops - 1)
+        gather.use_side(hops - 1, apply)
+    gather.side_in(grid.outer - 1)
+    gather.use_side(grid.outer - 1, apply)
+    times_whole(ref.attn, ref.gathered_late, ref.hdot_late, rows)
+
+    def scores_late(here, tile):
+        hdot = ref.hdot_late[here, :]
+        ref.part_late[here, :TAGS] = tag_scores(hdot, ref.gain[...], ref.tag[...])
+        ref.part_late[here, TAGS:] = columns_of(
+            high_low(jnp.sum(ref.h[here, :] * hdot, -1, keepdims=True))
+            + high_low(early_norm)
+            + high_low(product_sq),
+            tile,
+        )
+
+    over_tokens(tokens, scores_late)
+    exchange(
+        ref, False, ref.part_late, ref.got_late, ref.mixed_late, ref.packed_late, *[getattr(ref, n) for n in SWAP_B]
+    )
+    gather.finish()
+    for copy in sent:
+        copy.wait_send()
+    small = [
+        remote(ref.scalars, ref.scalars_in.at[d], ref.send_s.at[d], ref.recv_s.at[d], other, mp)
+        for d, other in enumerate(far)
+    ]
+    for copy in small:
+        copy.start()
+    tangent(ref, ref.packed_late, ref.hdot_late)
+    sent = reduce_rows(grid, ref.attn, ref.gdot, ref.twice, *[getattr(ref, n) for n in REDUCE_B])
+    sums = ref.scalars[...]
+    for d, copy in enumerate(small):
+        copy.wait_recv()
+        sums = sums + ref.scalars_in[d]
+    count = HQ * HD * D
+    norm_mean = (sums[0:1, 2:3] + sums[0:1, 3:4]) / count
+    product_mean = (sums[0:1, 4:5] + sums[0:1, 5:6]) / count
+    sigma = 2.0 * jnp.sqrt((product_mean + MEAN_EPS) / (norm_mean + MEAN_EPS))
+    keep = 1.0 - DAMP
+    ref.iterate[...] = (
+        (1.0 + keep * (1.0 + keep)) * ref.direction[...]
+        - ((1.0 + 2.0 * keep) / sigma) * ref.once[...]
+        + ref.twice[...] / sigma / sigma
+    )
+    for copy in sent + small:
+        copy.wait_send()
+
+
+GATHER_A = ["ga0", "ga1", "ga2", "ga3"]
+GATHER_B = ["gb0", "gb1", "gb2", "gb3"]
+SWAP_A = ["sa0", "sa1", "sa2", "sa3"]
+SWAP_B = ["sb0", "sb1", "sb2", "sb3"]
+REDUCE_A = ["ra%d" % i for i in range(10)]
+REDUCE_B = ["rb%d" % i for i in range(10)]
+
+
+def whole(size, ways, starts, tags, gain, tag, direction, query, key, value, stream, proj):
+    rows, cols = direction.shape
+    tokens = key.shape[0]
+    held = tokens // ways
+    scratch = {
+        "direction": pltpu.VMEM(direction.shape, F32),
+        "query": pltpu.VMEM(query.shape, BF16),
+        "key": pltpu.VMEM(key.shape, BF16),
+        "value": pltpu.VMEM(value.shape, BF16),
+        "stream": pltpu.VMEM(stream.shape, BF16),
+        "proj": pltpu.VMEM(proj.shape, BF16),
+        "src": pltpu.VMEM((rows, cols), BF16),
+        "src_late": pltpu.VMEM((rows, cols), BF16),
+        "gathered": pltpu.VMEM((rows * size, cols), BF16),
+        "gathered_late": pltpu.VMEM((rows * size, cols), BF16),
+        "mine": pltpu.VMEM(query.shape, BF16),
+        "attn": pltpu.VMEM((tokens, query.shape[1]), BF16),
+        "h": pltpu.VMEM((tokens, cols), F32),
+        "hdot": pltpu.VMEM((tokens, cols), F32),
+        "hdot_late": pltpu.VMEM((tokens, cols), F32),
+        "gdot": pltpu.VMEM((tokens, cols), BF16),
+        "once": pltpu.VMEM((rows, cols), F32),
+        "twice": pltpu.VMEM((rows, cols), F32),
+        "onehot": pltpu.VMEM((tokens, TAGS), F32),
+        "zval": pltpu.VMEM((held, TAGS), F32),
+        "rscale": pltpu.VMEM((held, TAGS), F32),
+        "scalars": pltpu.VMEM((8, TAGS), F32),
+        "scalars_in": pltpu.VMEM((size - 1, 8, TAGS), F32),
+        "part": pltpu.VMEM((tokens, 3 * TAGS), BF16),
+        "part_late": pltpu.VMEM((tokens, 2 * TAGS), BF16),
+        "got": pltpu.VMEM((ways - 1, held, 3 * TAGS), BF16),
+        "got_late": pltpu.VMEM((ways - 1, held, 2 * TAGS), BF16),
+        "mixed": pltpu.VMEM((held, 3 * TAGS), BF16),
+        "mixed_late": pltpu.VMEM((held, 3 * TAGS), BF16),
+        "packed": pltpu.VMEM((tokens, 3 * TAGS), BF16),
+        "packed_late": pltpu.VMEM((tokens, 3 * TAGS), BF16),
+        "loads": pltpu.SemaphoreType.DMA((6,)),
+        "local": pltpu.SemaphoreType.DMA((2,)),
+        "send_m": pltpu.SemaphoreType.DMA((ways,)),
+        "recv_m": pltpu.SemaphoreType.DMA((ways,)),
+        "send_s": pltpu.SemaphoreType.DMA((size,)),
+        "recv_s": pltpu.SemaphoreType.DMA((size,)),
+    }
+    for group in (SWAP_A, SWAP_B):
+        scratch.update({name: pltpu.SemaphoreType.DMA((ways,)) for name in group})
+    for group in (GATHER_A, GATHER_B):
+        scratch.update(zip(group, gather_scratch(size)))
+    for group in (REDUCE_A, REDUCE_B):
+        scratch.update(zip(group, reduce_scratch(size, rows, cols)))
+    names = ["starts", "tags", "gain", "tag", "direction_in", "query_in", "key_in", "value_in"]
+    names += ["stream_in", "proj_in", "iterate"] + list(scratch)
     vmem = pl.BlockSpec(memory_space=pltpu.VMEM)
-    operands = (part, tags) if early else (part, tags) + state
-    out_shape = [jax.ShapeDtypeStruct((tokens, 3 * TAGS), BF16)]
-    if early:
-        out_shape += [jax.ShapeDtypeStruct((rows, TAGS), F32)] * 2
-    out_shape += [jax.ShapeDtypeStruct((8, TAGS), F32)]
-    sems = pltpu.SemaphoreType.DMA((ways,))
+    place = pl.BlockSpec(memory_space=pl.ANY)
     return pl.pallas_call(
-        functools.partial(curve_kernel, ways, early),
-        out_shape=tuple(out_shape),
-        in_specs=[vmem] * len(operands),
-        out_specs=(vmem,) * len(out_shape),
-        scratch_shapes=[
-            pltpu.VMEM((ways - 1, rows, width), BF16),
-            pltpu.VMEM((rows, 3 * TAGS), BF16),
-            sems,
-            sems,
-            sems,
-            sems,
-        ],
+        functools.partial(whole_kernel, size, names),
+        out_shape=jax.ShapeDtypeStruct((rows, cols), F32),
+        in_specs=[pl.BlockSpec(memory_space=pltpu.SMEM)] + [vmem] * 3 + [place] * 6,
+        out_specs=vmem,
+        scratch_shapes=list(scratch.values()),
         compiler_params=pltpu.CompilerParams(
-            collective_id=collective_id, has_side_effects=True, vmem_limit_bytes=VMEM_LIMIT
+            collective_id=0, has_side_effects=True, vmem_limit_bytes=VMEM_LIMIT
         ),
-        name="curve_early" if early else "curve_late",
-    )(*operands)
+        name="lissa",
+    )(starts, tags, gain, tag, direction, query, key, value, stream, proj)
 
 
 def reduce_rows(grid, attn, gdot, own, full, away, kept, from_x, out, from_z, s_x, r_x, s_z, r_z):
@@ -586,160 +725,10 @@
     ]
 
 
-REDUCE_REFS = 10
-
-
-def sum_gather_kernel(size, attn, gdot, own, hdot, gathered, mine, local, *refs):
-    grid = Grid(size)
-    greet(grid.peers())
-    sent = reduce_rows(grid, attn, gdot, own, *refs[:REDUCE_REFS])
-    mine[...] = own[...].astype(BF16)
-    gather = Gather(grid, mine, gathered, local.at[0], *refs[REDUCE_REFS:])
-    gather.start()
-    hdot[...] = jnp.zeros_like(hdot)
-    apply = times_shards(attn, gathered, hdot, own.shape[0])
-    gather.use(0, 0, apply)
-    for hops in range(1, grid.outer):
-        gather.line_in(hops)
-        gather.use(hops, 0, apply)
-        gather.side_in(hops - 1)
-        gather.use_side(hops - 1, apply)
-    gather.side_in(grid.outer - 1)
-    gather.use_side(grid.outer - 1, apply)
-    times_whole(attn, gathered, hdot, own.shape[0])
-    gather.finish()
-    for copy in sent:
-        copy.wait_send()
-
-
-def sum_gather(size, attn, gdot):
-    tokens, total = attn.shape
-    cols = gdot.shape[1]
-    rows = total // size
-    vmem = pl.BlockSpec(memory_space=pltpu.VMEM)
-    return pl.pallas_call(
-        functools.partial(sum_gather_kernel, size),
-        out_shape=(
-            jax.ShapeDtypeStruct((rows, cols), F32),
-            jax.ShapeDtypeStruct((tokens, cols), F32),
-        ),
-        in_specs=[vmem, vmem],
-        out_specs=(vmem, vmem),
-        scratch_shapes=[
-            pltpu.VMEM((total, cols), BF16),
-            pltpu.VMEM((rows, cols), BF16),
-            pltpu.SemaphoreType.DMA((1,)),
-        ]
-        + reduce_scratch(size, rows, cols)
-        + gather_scratch(size),
-        compiler_params=pltpu.CompilerParams(
-            collective_id=2, has_side_effects=True, vmem_limit_bytes=VMEM_LIMIT
-        ),
-        name="sum_and_gather",
-    )(attn, gdot)
-
-
-def sum_kernel(size, attn, gdot, scalars, own, scalar_sum, got, s2, r2, *refs):
-    grid = Grid(size)
-    others = [lax.rem(lax.axis_index("dp") + d, size) for d in range(1, size)]
-    greet([(other, grid.mp) for other in others])
-    small = [
-        remote(scalars, got.at[d], s2.at[d], r2.at[d], other, grid.mp) for d, other in enumerate(others)
-    ]
-    for copy in small:
-        copy.start()
-    sent = reduce_rows(grid, attn, gdot, own, *refs)
-    total = scalars[...]
-    for d, copy in enumerate(small):
-        copy.wait_recv()
-        total = total + got[d]
-    scalar_sum[...] = total
-    for copy in sent + small:
-        copy.wait_send()
-
-
-def sum_only(size, attn, gdot, scalars):
-    cols = gdot.shape[1]
-    rows = attn.shape[1] // size
-    vmem = pl.BlockSpec(memory_space=pltpu.VMEM)
-    return pl.pallas_call(
-        functools.partial(sum_kernel, size),
-        out_shape=(
-            jax.ShapeDtypeStruct((rows, cols), F32),
-            jax.ShapeDtypeStruct(scalars.shape, F32),
-        ),
-        in_specs=[vmem, vmem, vmem],
-        out_specs=(vmem, vmem),
-        scratch_shapes=[
-            pltpu.VMEM((size - 1,) + scalars.shape, F32),
-            pltpu.SemaphoreType.DMA((size - 1,)),
-            pltpu.SemaphoreType.DMA((size - 1,)),
-        ]
-        + reduce_scratch(size, rows, cols),
-        compiler_params=pltpu.CompilerParams(
-            collective_id=4, has_side_effects=True, vmem_limit_bytes=VMEM_LIMIT
-        ),
-        name="sum_rows",
-    )(attn, gdot, scalars)
-
-
-def split_columns(values, tokens):
-    out = []
-    for value in values:
-        value = jnp.broadcast_to(value, (tokens,))
-        high = lax.reduce_precision(value, 8, 7)
-        out += [high, value - high]
-    block = jnp.stack(out, -1).astype(BF16)
-    return jnp.pad(block, ((0, 0), (0, TAGS - len(out))))
-
-
 def local(size, ways, queries, keys, values, stream, out_proj, norm_gain, tag_proj, direction, starts, tags):
-    count = HQ * HD * D
-    tokens = keys.shape[1]
-    tag_column = tags[0][:, None]
-    attn, h_loc, hdot = first(
-        size, ways, starts, queries[0], keys[0], values[0], direction.astype(BF16), stream[0], out_proj
-    )
-    tag_twice = jnp.concatenate([tag_proj, tag_proj], 1)
-
-    def scores(value):
-        value = value * norm_gain
-        high = lax.reduce_precision(value, 8, 7)
-        low = (value - high).astype(BF16)
-        return (
-            jnp.dot(high.astype(BF16), tag_proj, preferred_element_type=F32)
-            + jnp.dot(low, tag_proj, preferred_element_type=F32)
-        ).astype(BF16)
-
-    def tangent(packed, hdot):
-        columns = packed[:, 2 * TAGS : 2 * TAGS + 4].astype(F32)
-        coeff = columns[:, 0:1] + columns[:, 1:2]
-        pull = columns[:, 2:3] + columns[:, 3:4]
-        back = lax.dot_general(
-            packed[:, : 2 * TAGS], tag_twice, (((1,), (1,)), ((), ())), preferred_element_type=F32
-        )
-        return (back * norm_gain - coeff * h_loc - pull * hdot).astype(BF16)
-
-    extra = split_columns([jnp.sum(h_loc * hdot, -1), jnp.sum(h_loc * h_loc, -1)], tokens)
-    part = jnp.concatenate([scores(h_loc), scores(hdot), extra], 1)
-    packed, zval, rscale, _ = curve(ways, part, tag_column, None, 1)
-    once, hdot = sum_gather(size, attn, tangent(packed, hdot))
-
-    extra = split_columns(
-        [jnp.sum(h_loc * hdot, -1), jnp.sum(direction * direction), jnp.sum(once * once)], tokens
-    )
-    part = jnp.concatenate([scores(hdot), extra], 1)
-    packed, scalars = curve(ways, part, tag_column, (zval, rscale), 3)
-    twice, sums = sum_only(size, attn, tangent(packed, hdot), scalars)
-
-    early_norm = sums[0, 2] + sums[0, 3]
-    product_sq = sums[0, 4] + sums[0, 5]
-    sigma = 2.0 * jnp.sqrt((product_sq / count + MEAN_EPS) / (early_norm / count + MEAN_EPS))
-    keep = 1.0 - DAMP
-    return (
-        (1.0 + keep * (1.0 + keep)) * direction
-        - ((1.0 + 2.0 * keep) / sigma) * once
-        + twice / sigma / sigma
+    return whole(
+        size, ways, starts, tags, norm_gain[None], tag_proj, direction,
+        queries[0], keys[0], values[0], stream[0], out_proj,
     )
 
 

time: 249 us -> 213 us (0.86)
  other arithmetic: 9.17 us -> 0 us
  between operations: 9.18 us -> 0.01 us
  local copies, waits for them, and re-layouts: 10.8 us -> 3.43 us
  matrix products: 6.85 us -> 0 us
  Pallas kernels: 212 us -> 209 us
    reduce_sum x4 -> x0, other arithmetic: 6.97 us -> none  [the longest x2 3.63 us: local(): jnp.sum(h_loc * hdot, -1)]
    dot_general x8 -> x0, matrix products: 6.85 us -> none  [the longest x3 4.49 us: scores(): jnp.dot(high.astype(BF16), tag_proj, preferred_element_type=F32)]
    unnamed x33 -> x1, local copies, waits for them, and re-layouts: 7.91 us -> 2.16 us
    pallas_call x5 -> x1, Pallas kernels: 212 us -> 209 us  [whole(): pl.pallas_call(functools.partial(whole_kernel, size, names), out_shape=ja...]
where the time goes in v4:
time: 213 us
  Pallas kernels  209 us (98%)
  local copies, waits for them, and re-layouts  3.43 us (2%)
    pallas_call x1, Pallas kernels, whole(): pl.pallas_call(functools.partial(whole_kernel, size, names), out_shape=ja...  209 us

profile of v4, /device:TPU:0, one launch (start us, length us, event | category | flops | bytes accessed | tf_op | source)
XLA Modules:
  0.0 212.7 jit_solution(14846380627035885734)
XLA Ops:
  0.0 1.3 broadcast_in_dim.3.refs_2_
  1.3 209.3 %lissa.1 = f32[256,896]{1,0:T(8,128)} custom-call(s32[1,4]{1,0:T(1,128)} %refs_0_.1, s32[1,512]{1,0:T(1,128)} %refs_1_.1, f32[1,896]{1,0:T(1,128)} %broadcast_in_dim.3.refs_2_, bf16[896,128]{1,0:T(8,128)(2,1)} %refs_3_.1, f32[256,896]{1,0:T(8,128)} %refs_4_.1, bf16[128,2048]{1,0:T(8,128)(2,1)} %bitcast.7, bf16[512,1024]{1,0:T(8,128)(2,1)} %bitcast.4, ...), custom_call_target="tpu_custom_call" | custom-call | tf_op jit(solution)/shard_map/lissa/pallas_call | solution.py:582
  210.6 2.2 %copy.12 = f32[256,896]{1,0:T(8,128)} copy(f32[256,896]{1,0:T(8,128)} %lissa.1) | data formatting | bytes 1835008

commit v5 on v4

--- a/solution.py
+++ b/solution.py
@@ -21,7 +21,6 @@
 
 MESH = pl.DeviceIdType.MESH
 VMEM_LIMIT = 58 * 1024 * 1024
-CHUNKS = 2
 STEPS = 4
 LANES = 128
 F32 = jnp.float32
@@ -70,9 +69,10 @@
         return out + [(self.at(0, dx), self.mp) for dx in range(1, self.inner)]
 
 
-def part_rows(ref, device, rows, chunk):
-    step = rows // CHUNKS
-    return ref.at[pl.ds(pl.multiple_of(device * rows + chunk * step, step), step)]
+def spans_of(rows):
+    first = max(16, rows // 8 // 16 * 16)
+    second = (rows - first) // 2 // 16 * 16
+    return [(0, first), (first, second), (first + second, rows - first - second)]
 
 
 class Gather:
@@ -84,11 +84,14 @@
         self.line = (send, recv)
         self.side = (send_x, recv_x)
         self.rows = src.shape[0]
+        self.spans = spans_of(self.rows)
+        self.started = 0
 
     def block(self, way, hops, dx, c):
         z = self.grid.z - hops * way
         x = lax.rem(self.grid.x + (dx + self.grid.inner), self.grid.inner)
-        return part_rows(self.dst, z * self.grid.inner + x, self.rows, c)
+        start, size = self.spans[c]
+        return self.dst.at[pl.ds(pl.multiple_of((z * self.grid.inner + x) * self.rows + start, 16), size)]
 
     def arrives(self, way, hops):
         return self.grid.z >= hops if way > 0 else self.grid.z + hops < self.grid.outer
@@ -96,12 +99,17 @@
     def goes_on(self, way):
         return self.grid.z < self.grid.outer - 1 if way > 0 else self.grid.z > 0
 
-    def hop(self, piece, way, hops, c):
+    def hop(self, piece, way, hops, dx, c):
         send, recv = self.line
         lane = (way + 1) // 2
         dp = (self.grid.z + way) * self.grid.inner + self.grid.x
         return remote(
-            piece, self.block(way, hops, 0, c), send.at[lane, hops, c], recv.at[lane, hops + 1, c], dp, self.grid.mp
+            piece,
+            self.block(way, hops, dx, c),
+            send.at[lane, hops, dx, c],
+            recv.at[lane, hops + 1, dx, c],
+            dp,
+            self.grid.mp,
         )
 
     def aside(self, piece, way, hops, dx, c):
@@ -117,47 +125,71 @@
         )
 
     def own(self, c):
-        step = self.rows // CHUNKS
-        return self.src.at[pl.ds(c * step, step)]
-
-    def start(self):
-        for c in range(CHUNKS):
-            for way in (1, -1):
-                pl.when(self.goes_on(way))(lambda way=way, c=c: self.hop(self.own(c), way, 0, c).start())
+        start, size = self.spans[c]
+        return self.src.at[pl.ds(start, size)]
+
+    def start(self, ready):
+        while self.started < len(self.spans) and sum(self.spans[self.started]) <= ready:
+            c = self.started
             for dx in range(1, self.grid.inner):
                 self.aside(self.own(c), 1, 0, dx, c).start()
+            for way in (1, -1):
+                pl.when(self.goes_on(way))(lambda way=way, c=c: self.hop(self.own(c), way, 0, 0, c).start())
+            self.started += 1
+
+    def keep(self):
         me = self.grid.at(0, 0)
         whole = self.dst.at[pl.ds(pl.multiple_of(me * self.rows, self.rows), self.rows)]
         kept = pltpu.make_async_copy(self.src, whole, self.local)
         kept.start()
         kept.wait()
 
+    def relay_first(self):
+        for dx in range(1, self.grid.inner):
+            back = self.grid.inner - dx
+            piece = self.block(1, 0, back, 0)
+            self.aside(piece, 1, 0, dx, 0).wait_recv()
+            for way in (1, -1):
+                pl.when(self.goes_on(way))(
+                    lambda way=way, piece=piece, back=back: self.hop(piece, way, 0, back, 0).start()
+                )
+
     def take(self, way, hops, c):
-        piece = self.block(way, hops, 0, c)
         lane = (way + 1) // 2
         send, recv = self.line
         dp = (self.grid.z - way) * self.grid.inner + self.grid.x
-        remote(piece, piece, send.at[lane, hops, c], recv.at[lane, hops, c], dp, self.grid.mp).wait_recv()
-        if hops < self.grid.outer - 1:
-            pl.when(self.goes_on(way))(lambda: self.hop(piece, way, hops, c).start())
-        for dx in range(1, self.grid.inner):
-            self.aside(piece, way, hops, dx, c).start()
+        for dx in range(1 if c else self.grid.inner):
+            piece = self.block(way, hops, dx, c)
+            remote(piece, piece, send.at[lane, hops, dx, c], recv.at[lane, hops, dx, c], dp, self.grid.mp).wait_recv()
+            if hops < self.grid.outer - 1:
+                pl.when(self.goes_on(way))(
+                    lambda piece=piece, dx=dx: self.hop(piece, way, hops, dx, c).start()
+                )
+        if c:
+            piece = self.block(way, hops, 0, c)
+            for dx in range(1, self.grid.inner):
+                self.aside(piece, way, hops, dx, c).start()
 
     def take_aside(self, way, hops, c):
-        for dx in range(1, self.grid.inner):
-            piece = self.block(way, hops, -dx, c)
-            self.aside(piece, way, hops, dx, c).wait_recv()
+        if c:
+            for dx in range(1, self.grid.inner):
+                piece = self.block(way, hops, -dx, c)
+                self.aside(piece, way, hops, dx, c).wait_recv()
 
     def settle(self, way, hops, c):
-        piece = self.own(c) if hops == 0 else self.block(way, hops, 0, c)
-        if hops < self.grid.outer - 1:
-            pl.when(self.goes_on(way))(lambda: self.hop(piece, way, hops, c).wait_send())
-        if hops or way > 0:
+        for dx in range(1 if c else self.grid.inner):
+            piece = self.own(c) if hops == 0 and dx == 0 else self.block(way, hops, dx, c)
+            if hops < self.grid.outer - 1:
+                pl.when(self.goes_on(way))(
+                    lambda piece=piece, dx=dx: self.hop(piece, way, hops, dx, c).wait_send()
+                )
+        if (c and hops) or (hops == 0 and way > 0):
+            piece = self.block(way, hops, 0, c) if hops else self.own(c)
             for dx in range(1, self.grid.inner):
                 self.aside(piece, way, hops, dx, c).wait_send()
 
     def each(self, act, hops):
-        for c in range(CHUNKS):
+        for c in range(len(self.spans)):
             for way in (1, -1):
                 pl.when(self.arrives(way, hops))(lambda way=way, c=c: act(way, hops, c))
 
@@ -168,7 +200,7 @@
         if hops:
             self.each(self.take_aside, hops)
         else:
-            for c in range(CHUNKS):
+            for c in range(len(self.spans)):
                 self.take_aside(1, 0, c)
 
     def use(self, hops, dx, apply):
@@ -186,17 +218,15 @@
             if hops:
                 self.each(self.settle, hops)
             else:
-                for c in range(CHUNKS):
+                for c in range(len(self.spans)):
                     for way in (1, -1):
                         self.settle(way, 0, c)
 
 
 def gather_scratch(size):
     inner = inner_of(size)
-    outer = size // inner
-    line = pltpu.SemaphoreType.DMA((2, outer, CHUNKS))
-    side = pltpu.SemaphoreType.DMA((2, outer, inner, CHUNKS))
-    return [line, line, side, side]
+    sems = pltpu.SemaphoreType.DMA((2, size // inner, inner, 3))
+    return [sems] * 4
 
 
 def times_shards(attn, gathered, out, rows):
@@ -392,11 +422,13 @@
     loading[0].wait()
     ref.src[...] = ref.direction[...].astype(BF16)
     gather = Gather(grid, ref.src, ref.gathered, ref.local.at[0], *[getattr(ref, n) for n in GATHER_A])
-    gather.start()
+    gather.start(rows)
+    gather.keep()
     for copy in loading[1:4]:
         copy.wait()
 
     def between():
+        gather.relay_first()
         if grid.outer > 1:
             gather.line_in(1)
 
@@ -413,6 +445,7 @@
         copy.start()
     own = pltpu.make_async_copy(ref.mine, rows_of(mp), ref.local.at[1])
     own.start()
+    ref.gain[...] = ref.gain_in[...].reshape(1, ref.gain.shape[1])
     tag_ids = lax.broadcasted_iota(jnp.int32, (TAGS, tokens), 0)
     ref.onehot[...] = jnp.transpose((tag_ids == ref.tags[...]).astype(F32))
     ref.hdot[...] = jnp.zeros_like(ref.hdot)
@@ -457,12 +490,17 @@
     for copy in sent:
         copy.wait_send()
     tangent(ref, ref.packed, ref.hdot)
-    sent = reduce_rows(grid, ref.attn, ref.gdot, ref.once, *[getattr(ref, n) for n in REDUCE_A])
-    ref.src_late[...] = ref.once[...].astype(BF16)
     gather = Gather(
         grid, ref.src_late, ref.gathered_late, ref.local.at[0], *[getattr(ref, n) for n in GATHER_B]
     )
-    gather.start()
+
+    def done(here, ready):
+        ref.src_late[here, :] = ref.once[here, :].astype(BF16)
+        gather.start(ready)
+
+    sent = reduce_rows(grid, ref.attn, ref.gdot, ref.once, done, *[getattr(ref, n) for n in REDUCE_A])
+    gather.keep()
+    gather.relay_first()
     product_sq = jnp.sum(ref.once[...] * ref.once[...], keepdims=True)
     apply = times_shards(ref.attn, ref.gathered_late, ref.hdot_late, rows)
     gather.use(0, 0, apply)
@@ -499,7 +537,7 @@
     for copy in small:
         copy.start()
     tangent(ref, ref.packed_late, ref.hdot_late)
-    sent = reduce_rows(grid, ref.attn, ref.gdot, ref.twice, *[getattr(ref, n) for n in REDUCE_B])
+    sent = reduce_rows(grid, ref.attn, ref.gdot, ref.twice, None, *[getattr(ref, n) for n in REDUCE_B])
     sums = ref.scalars[...]
     for d, copy in enumerate(small):
         copy.wait_recv()
@@ -510,9 +548,7 @@
     sigma = 2.0 * jnp.sqrt((product_mean + MEAN_EPS) / (norm_mean + MEAN_EPS))
     keep = 1.0 - DAMP
     ref.iterate[...] = (
-        (1.0 + keep * (1.0 + keep)) * ref.direction[...]
-        - ((1.0 + 2.0 * keep) / sigma) * ref.once[...]
-        + ref.twice[...] / sigma / sigma
+        ref.twice[...] / sigma / sigma - ((1.0 + 2.0 * keep) / sigma) * ref.once[...]
     )
     for copy in sent + small:
         copy.wait_send()
@@ -531,6 +567,7 @@
     tokens = key.shape[0]
     held = tokens // ways
     scratch = {
+        "gain": pltpu.VMEM((1, cols), F32),
         "direction": pltpu.VMEM(direction.shape, F32),
         "query": pltpu.VMEM(query.shape, BF16),
         "key": pltpu.VMEM(key.shape, BF16),
@@ -575,7 +612,7 @@
         scratch.update(zip(group, gather_scratch(size)))
     for group in (REDUCE_A, REDUCE_B):
         scratch.update(zip(group, reduce_scratch(size, rows, cols)))
-    names = ["starts", "tags", "gain", "tag", "direction_in", "query_in", "key_in", "value_in"]
+    names = ["starts", "tags", "gain_in", "tag", "direction_in", "query_in", "key_in", "value_in"]
     names += ["stream_in", "proj_in", "iterate"] + list(scratch)
     vmem = pl.BlockSpec(memory_space=pltpu.VMEM)
     place = pl.BlockSpec(memory_space=pl.ANY)
@@ -592,7 +629,7 @@
     )(starts, tags, gain, tag, direction, query, key, value, stream, proj)
 
 
-def reduce_rows(grid, attn, gdot, own, full, away, kept, from_x, out, from_z, s_x, r_x, s_z, r_z):
+def reduce_rows(grid, attn, gdot, own, done, full, away, kept, from_x, out, from_z, s_x, r_x, s_z, r_z):
     rows, cols = own.shape
     step = rows // STEPS
     outer, inner = grid.outer, grid.inner
@@ -705,6 +742,9 @@
                     came, came, s_z.at[0, c], r_z.at[lane, 0, c], side * inner + grid.x, grid.mp
                 ).wait_recv()
                 piece(own, c)[...] += came[...].astype(F32)
+
+        if done is not None:
+            done(pl.ds(c * step, step), (c + 1) * step)
     return sent
 
 
@@ -726,10 +766,12 @@
 
 
 def local(size, ways, queries, keys, values, stream, out_proj, norm_gain, tag_proj, direction, starts, tags):
-    return whole(
-        size, ways, starts, tags, norm_gain[None], tag_proj, direction,
+    moved = whole(
+        size, ways, starts, tags, norm_gain, tag_proj, direction,
         queries[0], keys[0], values[0], stream[0], out_proj,
     )
+    keep = 1.0 - DAMP
+    return (1.0 + keep * (1.0 + keep)) * direction + moved
 
 
 def solution(mesh):

time: 213 us -> 216 us (1.014)
  Pallas kernels: 209 us -> 213 us
  local copies, waits for them, and re-layouts: 3.43 us -> 0.01 us
  other arithmetic: 0 us -> 2.21 us
    pallas_call x1, Pallas kernels: 209 us -> 213 us  [whole(): pl.pallas_call(functools.partial(whole_kernel, size, names), out_shape=ja...]
    add x0 -> x1, other arithmetic: none -> 2.21 us  [local(): return (1.0 + keep * (1.0 + keep)) * direction + moved]
where the time goes in v5:
time: 216 us; the launch traced here: 215 us
  Pallas kernels  213 us (99%)
  other arithmetic  2.21 us (1%)
    pallas_call x1, Pallas kernels, whole(): pl.pallas_call(functools.partial(whole_kernel, size, names), out_shape=ja...  213 us

profile of v5, /device:TPU:0, one launch (start us, length us, event | category | flops | bytes accessed | tf_op | source)
XLA Modules:
  0.0 215.4 jit_solution(8719320117088603336)
XLA Ops:
  0.0 0.0 copy-start
  0.0 213.2 %lissa.1 = f32[256,896]{1,0:T(8,128)} custom-call(s32[1,4]{1,0:T(1,128)} %refs_0_.1, s32[1,512]{1,0:T(1,128)} %refs_1_.1, f32[896]{0:T(1024)} %refs_2_.1, bf16[896,128]{1,0:T(8,128)(2,1)} %refs_3_.1, f32[256,896]{1,0:T(8,128)} %refs_4_.1, bf16[128,2048]{1,0:T(8,128)(2,1)} %bitcast.7, bf16[512,1024]{1,0:T(8,128)(2,1)} %bitcast.4, bf16[512,1024]{1,0:T(8,128)(2,1)} %bitcast.5, ...), custom_call_target="tpu_custom_call" | custom-call | tf_op jit(solution)/shard_map/lissa/pallas_call | solution.py:619
  213.2 0.0 copy-done
  213.2 2.2 %multiply_add_fusion = f32[256,896]{1,0:T(8,128)} fusion(f32[256,896]{1,0:T(8,128)} %lissa.1, f32[256,896]{1,0:T(8,128)S(1)} %copy-done), kind=kLoop, calls=%fused_computation | loop fusion | flops 458752 | bytes 2752512 | tf_op jit(solution)/shard_map/add | solution.py:774
Async XLA Ops:
  0.0 213.2 %copy-start = (f32[256,896]{1,0:T(8,128)S(1)}, f32[256,896]{1,0:T(8,128)}, u32[]{:S(2)}) copy-start(f32[256,896]{1,0:T(8,128)} %refs_4_.1) | copy-start | bytes 2752516

commit v6 on v4

--- a/solution.py
+++ b/solution.py
@@ -405,14 +405,21 @@
     def rows_of(device):
         return ref.attn.at[pl.ds(pl.multiple_of(device * q_rows, q_rows), q_rows)]
 
-    sent = [
-        remote(ref.mine, rows_of(mp), ref.send_m.at[d], ref.recv_m.at[d], dp, other)
-        for d, other in enumerate(others)
+    half = ways // 2
+    sibling = mp + 1 - 2 * lax.rem(mp, 2)
+
+    def alike(hops, core):
+        return lax.rem(mp // 2 + (half - hops), half) * 2 + lax.rem(core, 2)
+
+    sent = [remote(ref.mine, rows_of(mp), ref.send_m.at[0], ref.recv_m.at[0], dp, sibling)] + [
+        remote(ref.mine, rows_of(mp), ref.send_m.at[d], ref.recv_m.at[d], dp, alike(half - d, mp))
+        for d in range(1, half)
     ]
     for copy in sent:
         copy.start()
     own = pltpu.make_async_copy(ref.mine, rows_of(mp), ref.local.at[1])
     own.start()
+    ref.gain[...] = ref.gain_in[...].reshape(1, ref.gain.shape[1])
     tag_ids = lax.broadcasted_iota(jnp.int32, (TAGS, tokens), 0)
     ref.onehot[...] = jnp.transpose((tag_ids == ref.tags[...]).astype(F32))
     ref.hdot[...] = jnp.zeros_like(ref.hdot)
@@ -421,9 +428,16 @@
     for hops in range(2, grid.outer):
         gather.line_in(hops)
     own.wait()
-    for d, other in enumerate(others):
-        place = rows_of(lax.rem(mp + (ways - 1 - d), ways))
-        remote(place, place, ref.send_m.at[d], ref.recv_m.at[d], dp, other).wait_recv()
+    for d in range(1, half):
+        place = rows_of(alike(d, mp))
+        remote(place, place, ref.send_m.at[d], ref.recv_m.at[d], dp, sibling).wait_recv()
+        copy = remote(place, place, ref.send_m.at[half + d], ref.recv_m.at[half + d], dp, sibling)
+        copy.start()
+        sent.append(copy)
+    for d in range(half):
+        place = rows_of(alike(d, mp + 1))
+        slot = half + d if d else 0
+        remote(place, place, ref.send_m.at[slot], ref.recv_m.at[slot], dp, sibling).wait_recv()
     for copy in loading[4:]:
         copy.wait()
 
@@ -531,6 +545,7 @@
     tokens = key.shape[0]
     held = tokens // ways
     scratch = {
+        "gain": pltpu.VMEM((1, cols), F32),
         "direction": pltpu.VMEM(direction.shape, F32),
         "query": pltpu.VMEM(query.shape, BF16),
         "key": pltpu.VMEM(key.shape, BF16),
@@ -575,7 +590,7 @@
         scratch.update(zip(group, gather_scratch(size)))
     for group in (REDUCE_A, REDUCE_B):
         scratch.update(zip(group, reduce_scratch(size, rows, cols)))
-    names = ["starts", "tags", "gain", "tag", "direction_in", "query_in", "key_in", "value_in"]
+    names = ["starts", "tags", "gain_in", "tag", "direction_in", "query_in", "key_in", "value_in"]
     names += ["stream_in", "proj_in", "iterate"] + list(scratch)
     vmem = pl.BlockSpec(memory_space=pltpu.VMEM)
     place = pl.BlockSpec(memory_space=pl.ANY)
@@ -727,7 +742,7 @@
 
 def local(size, ways, queries, keys, values, stream, out_proj, norm_gain, tag_proj, direction, starts, tags):
     return whole(
-        size, ways, starts, tags, norm_gain[None], tag_proj, direction,
+        size, ways, starts, tags, norm_gain, tag_proj, direction,
         queries[0], keys[0], values[0], stream[0], out_proj,
     )
 

time: 213 us -> 210 us (0.986)
  no operation moved by 1% of the time
where the time goes in v6:
time: 210 us
  Pallas kernels  207 us (99%)
  local copies, waits for them, and re-layouts  2.16 us (1%)
    pallas_call x1, Pallas kernels, whole(): pl.pallas_call(functools.partial(whole_kernel, size, names), out_shape=ja...  207 us

profile of v6, /device:TPU:0, one launch (start us, length us, event | category | flops | bytes accessed | tf_op | source)
XLA Modules:
  0.0 209.5 jit_solution(16640963721341949613)
XLA Ops:
  0.0 207.4 %lissa.1 = f32[256,896]{1,0:T(8,128)} custom-call(s32[1,4]{1,0:T(1,128)} %refs_0_.1, s32[1,512]{1,0:T(1,128)} %refs_1_.1, f32[896]{0:T(1024)} %refs_2_.1, bf16[896,128]{1,0:T(8,128)(2,1)} %refs_3_.1, f32[256,896]{1,0:T(8,128)} %refs_4_.1, bf16[128,2048]{1,0:T(8,128)(2,1)} %bitcast.7, bf16[512,1024]{1,0:T(8,128)(2,1)} %bitcast.4, bf16[512,1024]{1,0:T(8,128)(2,1)} %bitcast.5, ...), custom_call_target="tpu_custom_call" | custom-call | tf_op jit(solution)/shard_map/lissa/pallas_call | solution.py:597
  207.4 2.2 %copy.12 = f32[256,896]{1,0:T(8,128)} copy(f32[256,896]{1,0:T(8,128)} %lissa.1) | data formatting | bytes 1835008
